TPU v7x, 32 devices: a whole 2x2x4 slice. The times are simulated.
32 devices in a mesh: dp: 8 (over z, y), tensor: 4 (over x, core).
Axes of the slice: x: 2, y: 2, z: 4, core: 2. Of those that a mesh axis runs over, the one named last changes fastest.
Arguments:
- picture_averaged_encodings: bfloat16 [1536, 1152], P('dp'), may hold values from -6 to 6
- caption_averaged_encodings: bfloat16 [1536, 1152], P('dp'), may hold values from -6 to 6
- picture_mapping_matrix: bfloat16 [1152, 1152], P(None, 'tensor'), may hold values from -0.1875 to 0.1875
- caption_mapping_matrix: bfloat16 [1152, 1152], P(None, 'tensor'), may hold values from -0.1875 to 0.1875
- picture_weight_perturbation: bfloat16 [1152, 1152], P(None, 'tensor'), may hold values from -0.1875 to 0.1875
- caption_weight_perturbation: bfloat16 [1152, 1152], P(None, 'tensor'), may hold values from -0.1875 to 0.1875
- sharpness_multiplier: float32 [1], replicated, may hold values from 6 to 14
- offset_additive: float32 [1], replicated, may hold values from -8 to -4
Outputs:
- image_hvp: float32 [1152, 1152], P('dp', 'tensor')
- text_hvp: float32 [1152, 1152], P('dp', 'tensor')
All inputs are finite; a program needn't handle non-finite values.
Results may differ from a plain program's by a relative error of at most 0.0025.
Values may be sent and summed in bfloat16 or wider, within the bound.
No kernel may reach another device: no remote copies, remote signals or barrier semaphores. Data moves between devices by JAX's collectives and lax.ppermute only.
A program may use at most 128 MiB of HBM per device.

v0:
```python
import functools

import jax
import jax.numpy as jnp
from jax import lax
from jax.experimental import pallas as pl
from jax.experimental.pallas import tpu as pltpu
from jax.sharding import PartitionSpec as P

EPS = 1e-06


def swapped(value, axis, mask):
    count = lax.axis_size(axis)
    return lax.ppermute(value, axis, [(source, source ^ mask) for source in range(count)])


def matmul(left, right):
    return jnp.dot(left, right, preferred_element_type=jnp.float32)


def matmul_nt(left, right):
    return lax.dot_general(
        left, right, (((1,), (1,)), ((), ())), preferred_element_type=jnp.float32
    )


def matmul_tn(left, right):
    return lax.dot_general(
        left, right, (((0,), (0,)), ((), ())), preferred_element_type=jnp.float32
    )


def unit_parts(raw, raw_rate):
    values = raw.astype(jnp.float32)
    tangent = raw_rate.astype(jnp.float32)
    radius = jnp.sqrt(jnp.sum(values * values, axis=1, keepdims=True) + EPS)
    unit = values / radius
    rate = jnp.sum(unit * tangent, axis=1, keepdims=True)
    unit_tangent = (tangent - unit * rate) / radius
    return (unit, unit_tangent, radius, rate)


def unit_backward(unit, unit_tangent, radius, rate, grad, grad_rate):
    inner = jnp.sum(unit * grad, axis=1, keepdims=True)
    inner_rate = jnp.sum(unit_tangent * grad + unit * grad_rate, axis=1, keepdims=True)
    first = (grad - unit * inner) / radius
    return (grad_rate - unit_tangent * inner - unit * inner_rate - first * rate) / radius


def general(
    picture_averaged_encodings,
    caption_averaged_encodings,
    picture_mapping_matrix,
    caption_mapping_matrix,
    picture_weight_perturbation,
    caption_weight_perturbation,
    sharpness_multiplier,
    offset_additive,
):
    similarity_multiplier = sharpness_multiplier[0]
    logit_bias = offset_additive[0]
    tensor_rank = lax.axis_index("tensor")
    data_rank = lax.axis_index("dp")
    tensor_count = lax.axis_size("tensor")
    data_count = lax.axis_size("dp")
    planes = data_count // 2
    rows, width = picture_averaged_encodings.shape
    cols = picture_mapping_matrix.shape[1]
    share = rows // tensor_count
    out_rows = width // data_count
    half = jnp.bfloat16

    text = jnp.stack(
        [
            matmul(caption_averaged_encodings, caption_mapping_matrix).astype(half),
            matmul(caption_averaged_encodings, caption_weight_perturbation).astype(half),
        ]
    )
    image = jnp.stack(
        [
            matmul(picture_averaged_encodings, picture_mapping_matrix).astype(half),
            matmul(picture_averaged_encodings, picture_weight_perturbation).astype(half),
        ]
    )

    def share_of(value, axis, mask):
        start = (tensor_rank ^ mask) * share
        return lax.dynamic_slice_in_dim(value, start, share, axis)

    parts = [share_of(text, 1, 0)]
    for mask in range(1, tensor_count):
        parts.append(swapped(share_of(text, 1, mask), "tensor", mask))
    text = jnp.concatenate(parts, axis=2)
    slots = [text] + [swapped(text, "dp", 2 * mask) for mask in range(1, planes)]

    image = jnp.concatenate([image, swapped(image, "dp", 1)], axis=1)
    blocks = [image]
    mask = tensor_count // 2
    image_blocks = {0: image}
    while mask >= 1:
        held = sorted(image_blocks)
        sent = jnp.concatenate([image_blocks[k] for k in held], axis=2)
        got = swapped(sent, "tensor", mask)
        for place, k in enumerate(held):
            image_blocks[k ^ mask] = got[:, :, place * cols : (place + 1) * cols]
        mask //= 2
    image = jnp.concatenate([image_blocks[k] for k in range(tensor_count)], axis=2)
    text = jnp.concatenate(slots, axis=1)

    def out_columns(value, rank):
        taken = [
            lax.dynamic_slice_in_dim(value, (rank ^ (2 * mask)) * out_rows, out_rows, 1)
            for mask in range(planes)
        ]
        return jnp.concatenate(taken, axis=1)

    def plane_encodings(value):
        other = swapped(out_columns(value, data_rank ^ 1), "dp", 1)
        return jnp.concatenate([out_columns(value, data_rank), other], axis=0)

    picture_plane = plane_encodings(picture_averaged_encodings)
    ordered = jnp.concatenate(
        [share_of(caption_averaged_encodings, 0, mask) for mask in range(tensor_count)], axis=0
    )
    caption_plane = plane_encodings(ordered)

    image_unit, image_tangent, image_radius, image_rate = unit_parts(image[0], image[1])
    text_unit, text_tangent, text_radius, text_rate = unit_parts(text[0], text[1])
    image_half = image_unit.astype(half)
    image_tangent_half = image_tangent.astype(half)
    text_half = text_unit.astype(half)
    text_tangent_half = text_tangent.astype(half)

    logits = similarity_multiplier * matmul_nt(text_half, image_half) + logit_bias
    logit_rate = similarity_multiplier * (
        matmul_nt(text_half, image_tangent_half) + matmul_nt(text_tangent_half, image_half)
    )
    probability = jax.nn.sigmoid(logits)
    text_ids = lax.broadcasted_iota(jnp.int32, (logits.shape[0], 1), 0)
    image_ids = lax.broadcasted_iota(jnp.int32, (1, logits.shape[1]), 1)
    positive = ((text_ids < share) & (text_ids + tensor_rank * share == image_ids)).astype(
        jnp.float32
    )
    weight = (probability - positive).astype(half)
    weight_rate = (probability * (1.0 - probability) * logit_rate).astype(half)
    text_grad = similarity_multiplier * matmul(weight, image_half)
    text_grad_rate = similarity_multiplier * (
        matmul(weight_rate, image_half) + matmul(weight, image_tangent_half)
    )
    image_grad = similarity_multiplier * matmul_tn(weight, text_half)
    image_grad_rate = similarity_multiplier * (
        matmul_tn(weight_rate, text_half) + matmul_tn(weight, text_tangent_half)
    )

    text_back = unit_backward(
        text_unit, text_tangent, text_radius, text_rate, text_grad, text_grad_rate
    )
    image_back = unit_backward(
        image_unit, image_tangent, image_radius, image_rate, image_grad, image_grad_rate
    )

    total = text_back[:share]
    for mask in range(1, planes):
        sent = text_back[mask * share : (mask + 1) * share].astype(half)
        total = total + swapped(sent, "dp", 2 * mask).astype(jnp.float32)
    text_back = total.astype(half)
    parts = [text_back[:, :cols]]
    for mask in range(1, tensor_count):
        sent = text_back[:, mask * cols : (mask + 1) * cols]
        parts.append(swapped(sent, "tensor", mask))
    text_back = jnp.concatenate(parts, axis=0)
    text_back = jnp.concatenate([text_back, swapped(text_back, "dp", 1)], axis=0)

    image_blocks = {k: image_back[:, k * cols : (k + 1) * cols] for k in range(tensor_count)}
    mask = 1
    while mask < tensor_count:
        kept = [k for k in sorted(image_blocks) if not k & mask]
        sent = jnp.concatenate([image_blocks[k ^ mask] for k in kept], axis=1)
        got = swapped(sent, "tensor", mask).astype(jnp.float32)
        image_blocks = {
            k: image_blocks[k] + got[:, place * cols : (place + 1) * cols]
            for place, k in enumerate(kept)
        }
        mask *= 2
    image_back = image_blocks[0]
    got = swapped(image_back, "dp", 1)
    image_back = (
        image_back + jnp.concatenate([got[rows:], got[:rows]], axis=0)
    ).astype(half)

    def head(encodings, back):
        product = matmul_tn(encodings, back)
        total = product[:out_rows]
        for mask in range(1, planes):
            sent = product[mask * out_rows : (mask + 1) * out_rows].astype(half)
            total = total + swapped(sent, "dp", 2 * mask).astype(jnp.float32)
        return total

    return (head(picture_plane, image_back), head(caption_plane, text_back))


def call(kernel, outs, *args, after=(), scratch=()):
    count = len(args)

    def body(*refs):
        kernel(*refs[:count], *refs[count + len(after) :])

    def place(value):
        scalar = value.ndim == 1
        return pl.BlockSpec(memory_space=pltpu.SMEM if scalar else pltpu.VMEM)

    return pl.pallas_call(
        body,
        out_shape=[jax.ShapeDtypeStruct(shape, dtype) for shape, dtype in outs],
        in_specs=[place(value) for value in args]
        + [pl.BlockSpec(memory_space=pl.ANY) for _ in after],
        out_specs=[pl.BlockSpec(memory_space=pltpu.VMEM) for _ in outs],
        scratch_shapes=[pltpu.VMEM(shape, dtype) for shape, dtype in scratch],
        compiler_params=pltpu.CompilerParams(vmem_limit_bytes=48 * 1024 * 1024),
    )(*args, *after)


def folds(rows, main, tail):
    across = main // tail
    for k in range(rows // 16):
        here = slice(k * 16, (k + 1) * 16)
        at = rows + k // across * 16
        first = k % across * tail
        yield here, slice(at, at + 16), slice(first, first + tail)


def folded_rows(rows, main, tail):
    return rows + -(-rows // 16 // (main // tail)) * 16


def fold(out, first, value, main):
    rows, cols = value.shape
    out[first : first + rows, :] = value[:, :main].astype(out.dtype)
    for here, there, lanes in folds(rows, main, cols - main):
        there = slice(first + there.start, first + there.stop)
        out[there, lanes] = value[here, main:].astype(out.dtype)


def unfold(ref, first, rows, main, tail):
    tails = [
        ref[first + there.start : first + there.stop, lanes]
        for _, there, lanes in folds(rows, main, tail)
    ]
    return jnp.concatenate([ref[first : first + rows, :], jnp.concatenate(tails, axis=0)], axis=1)


def project_kernel(share, starts, encodings, weight, direction, *outs):
    main = weight.shape[0] // 128 * 128
    left = jnp.concatenate(
        [
            encodings[pl.ds(pl.multiple_of(starts[k], 16), share), :]
            for k in range(starts.shape[0])
        ],
        axis=0,
    )
    tails = jnp.concatenate([weight[main:, :], direction[main:, :]], axis=0)
    for right, first in ((weight[:main, :], 0), (direction[:main, :], main), (tails, 2 * main)):
        product = matmul_nt(left, right).astype(jnp.bfloat16)
        place = 0
        for out in outs:
            rows = out.shape[0]
            out[:, first : first + right.shape[0]] = product[place : place + rows]
            place += rows


def gathered(blocks, main, tail, which):
    first = 2 * main + which * tail
    mains = [block[:, which * main : (which + 1) * main] for block in blocks]
    tails = [block[:, first : first + tail] for block in blocks]
    return jnp.concatenate(mains + tails, axis=1)


def relay_kernel(mine, got, out):
    rows = mine.shape[0]
    out[:rows, :] = mine[...]
    out[rows:, :] = got[rows:, :]


def text_rows_kernel(main, tail, own, far, near, out):
    rows, width = own.shape[0], out.shape[1] // 2
    parts = (own[...], near[:rows, :], far[:rows, :], near[rows:, :])
    blocks = [part.astype(jnp.float32) for part in parts]
    out[:, :width] = gathered(blocks, main, tail, 0).astype(jnp.bfloat16)
    out[:, width:] = gathered(blocks, main, tail, 1).astype(jnp.bfloat16)


def row_factors(values, tangent):
    squares = jnp.sum(values * values, axis=1, keepdims=True)
    cross = jnp.sum(values * tangent, axis=1, keepdims=True)
    inverse = 1.0 / jnp.sqrt(squares + EPS)
    return inverse, cross * inverse


def unit_rows(values, tangent, inverse, rate):
    unit = values * inverse
    return unit, (tangent - unit * rate) * inverse


def back_rows(unit, tangent, inverse, rate, grad, grad_rate):
    inner = jnp.sum(unit * grad, axis=1, keepdims=True)
    inner_rate = jnp.sum(tangent * grad + unit * grad_rate, axis=1, keepdims=True)
    scaled = rate * inverse
    return (
        grad_rate - tangent * inner - grad * scaled + unit * (inner * scaled - inner_rate)
    ) * inverse


STEP = 48


def image_rows_kernel(main, tail, count, near, far, unit, tangent, half, tangent_half, factors):
    rows = unit.shape[0] // 2
    for shard in range(2):
        held = [
            (near, far)[k % 2].at[pl.ds((k - k % 2 + shard) * rows, rows), :] for k in range(count)
        ]

        @pl.loop(0, rows // STEP)
        def _(step):
            here = pl.ds(pl.multiple_of(step * STEP, STEP), STEP)
            there = pl.ds(pl.multiple_of(shard * rows + step * STEP, STEP), STEP)
            parts = [block[here, :].astype(jnp.float32) for block in held]
            values = gathered(parts, main, tail, 0)
            rates = gathered(parts, main, tail, 1)
            inverse, rate = row_factors(values, rates)
            one, two = unit_rows(values, rates, inverse, rate)
            unit[there, :] = one
            tangent[there, :] = two
            half[there, :] = one.astype(jnp.bfloat16)
            tangent_half[there, :] = two.astype(jnp.bfloat16)
            factors[0, there, :] = jnp.broadcast_to(inverse, (STEP, 128))
            factors[1, there, :] = jnp.broadcast_to(rate, (STEP, 128))


def text_rows(text):
    width = text.shape[1] // 2
    values, rates = text[:, :width].astype(jnp.float32), text[:, width:].astype(jnp.float32)
    inverse, rate = row_factors(values, rates)
    return unit_rows(values, rates, inverse, rate) + (inverse, rate)


def weight_kernel(slots, start, scalars, half, tangent_half, *refs):
    texts, outs = refs[:slots], refs[slots:]
    text_half, text_tangent_half, weight, weight_rate, weight_turned, weight_rate_turned = outs
    bf16 = jnp.bfloat16
    share = texts[0].shape[0]
    multiplier, bias = scalars[0], scalars[1]
    for slot, text in enumerate(texts):
        here = slice(slot * share, (slot + 1) * share)
        unit, tangent, _, _ = text_rows(text)
        text_half[here, :] = unit.astype(bf16)
        text_tangent_half[here, :] = tangent.astype(bf16)
    logits = multiplier * matmul_nt(text_half[...], half[...]) + bias
    logit_rate = multiplier * (
        matmul_nt(text_half[...], tangent_half[...])
        + matmul_nt(text_tangent_half[...], half[...])
    )
    probability = jax.nn.sigmoid(logits)
    text_ids = lax.broadcasted_iota(jnp.int32, logits.shape, 0)
    image_ids = lax.broadcasted_iota(jnp.int32, logits.shape, 1)
    positive = jnp.where((text_ids < share) & (text_ids + start[0] == image_ids), 1.0, 0.0)
    value = probability - positive
    value_rate = probability * (1.0 - probability) * logit_rate
    weight[...] = value.astype(bf16)
    weight_rate[...] = value_rate.astype(bf16)
    weight_turned[...] = value.T.astype(bf16)
    weight_rate_turned[...] = value_rate.T.astype(bf16)


def text_block_kernel(slots, scalars, half, tangent_half, weight, weight_rate, *refs):
    texts, sums = refs[:slots], refs[slots:]
    share = texts[0].shape[0]
    multiplier = scalars[0]
    grad = multiplier * matmul(weight[...], half[...])
    grad_rate = multiplier * (
        matmul(weight_rate[...], half[...]) + matmul(weight[...], tangent_half[...])
    )
    for slot, text in enumerate(texts):
        here = slice(slot * share, (slot + 1) * share)
        back = back_rows(*text_rows(text), grad[here], grad_rate[here])
        if slot % 2 == 0:
            sums[slot // 2][...] = back
        else:
            at = slice(slot // 2 * share, (slot // 2 + 1) * share)
            sums[2][at, :] = back.astype(jnp.bfloat16)


def forward_kernel(own, middle, got, total, sent):
    share = own.shape[0]
    total[...] = own[...] + got[:share, :].astype(jnp.float32)
    sent[...] = (middle[...] + got[share:, :].astype(jnp.float32)).astype(jnp.bfloat16)


def image_block_kernel(
    main,
    tail,
    scalars,
    unit,
    tangent,
    factors,
    text_half,
    text_tangent_half,
    weight,
    weight_rate,
    kept,
    sent,
):
    rows = unit.shape[0] // 2
    count = 4
    multiplier = scalars[0]
    for shard in range(2):
        here = slice(shard * rows, (shard + 1) * rows)
        grad = multiplier * matmul(weight[here, :], text_half[...])
        grad_rate = multiplier * (
            matmul(weight_rate[here, :], text_half[...])
            + matmul(weight[here, :], text_tangent_half[...])
        )
        back = back_rows(
            unit[here, :],
            tangent[here, :],
            factors[0, here, :1],
            factors[1, here, :1],
            grad,
            grad_rate,
        )
        for k in range(count):
            out = (kept, sent)[k % 2]
            to = slice(k // 2 * rows, (k // 2 + 1) * rows)
            out[to, shard * main : (shard + 1) * main] = back[:, k * main : (k + 1) * main]
            first = 2 * main + shard * tail
            taken = count * main + k * tail
            out[to, first : first + tail] = back[:, taken : taken + tail]


def text_sum_kernel(main, tail, own, *refs):
    count = own.shape[1] // (main + tail)
    got, outs = refs[:-count], refs[-count:]
    total = own[...]
    for ref in got:
        total = total + ref[...].astype(jnp.float32)
    for k, out in enumerate(outs):
        first = count * main + k * tail
        out[:, :main] = total[:, k * main : (k + 1) * main].astype(jnp.bfloat16)
        out[:, main:] = total[:, first : first + tail].astype(jnp.bfloat16)


def stack_kernel(*refs):
    rows = refs[0].shape[0]
    for k, ref in enumerate(refs[:-1]):
        refs[-1][k * rows : (k + 1) * rows, : ref.shape[1]] = ref[...]


def fold_kernel(*refs):
    value = jnp.concatenate([ref[...] for ref in refs[:-1]], axis=0)
    fold(refs[-1], 0, value, refs[-1].shape[1])


def turn_kernel(places, core, picture, caption, mine, other):
    for which, encodings in enumerate((picture, caption)):
        turned = encodings[...].astype(jnp.float32).T.astype(jnp.bfloat16)
        count = places.shape[0]
        size, rows = turned.shape[0] // count, turned.shape[1]
        fold = count // 4
        for block in range(count):
            taken = turned[block * size : (block + 1) * size, :]
            slot = places[block]
            at = pl.multiple_of(slot % fold * size, 16)
            for half in range(2):
                lanes = slice(half * rows, (half + 1) * rows)

                @pl.when(slot // fold == half)
                def _():
                    mine[pl.ds(which * fold * size + at, size), lanes] = taken

                @pl.when((slot // fold == 2 + half) & (core[0] == which))
                def _():
                    other[pl.ds(at, size), lanes] = taken


def shard_columns(value, main, tail, shard):
    at = 2 * main + shard * tail
    return jnp.concatenate(
        [value[:, shard * main : (shard + 1) * main], value[:, at : at + tail]], axis=1
    )


def image_pair_kernel(main, tail, share, near, kept, got, total, over_x, over_y, over_both):
    rows = total.shape[0]
    ours = kept[:rows, :] + got[:rows, :]
    theirs = kept[rows:, :] + got[rows:, :]
    total[...] = shard_columns(ours, main, tail, 0)
    fold(over_y, 0, shard_columns(ours, main, tail, 1), main)
    fold(over_both, 0, shard_columns(theirs, main, tail, 1), main)
    value = shard_columns(theirs, main, tail, 0)
    rounded = value.astype(jnp.bfloat16)
    fold(over_x, 0, rounded, main)
    left = value - rounded.astype(jnp.float32)
    left = jnp.where(near[0] == 0, left[: 2 * share], left[2 * share : 4 * share])
    fold(over_x, folded_rows(rows, main, tail), left, main)


def image_sum_kernel(main, tail, share, near, total, over_x, over_y, over_both, out):
    rows = total.shape[0]
    value = total[...]
    for source in (over_x, over_y, over_both):
        value = value + unfold(source, 0, rows, main, tail).astype(jnp.float32)
    left = unfold(over_x, folded_rows(rows, main, tail), 2 * share, main, tail)
    left = left.astype(jnp.float32)
    zero = jnp.zeros_like(left)
    far = near[0] == 0
    value = value + jnp.concatenate(
        [jnp.where(far, zero, left), jnp.where(far, left, zero)], axis=0
    )
    fold(out, 0, value.astype(jnp.bfloat16), main)


def head_kernel(main, tail, head, core, starts, mine, near, far, back, back_other, own, *refs):
    sent, (ordered,) = refs[:-1], refs[-1:]
    size, rows = own.shape[0], ordered.shape[1]
    share = rows // starts.shape[0]
    for which, ref in enumerate((back, back_other)):
        value = unfold(ref, 0, rows, main, tail)
        for k in range(starts.shape[0]):
            at = pl.ds(pl.multiple_of(starts[k], 16), share)
            ordered[which, at, :] = value[k * share : (k + 1) * share]
    count = (len(sent) + 1) // 2
    other = jnp.where(core[0] == head, near[...], far[...])
    for half in range(2):
        here = slice(head * count * size, (head + 1) * count * size)
        lanes = slice(half * rows, (half + 1) * rows)
        product = matmul(mine[here, lanes], ordered[0]) + matmul(other[:, lanes], ordered[1])
        for place in range(count):
            part = product[place * size : (place + 1) * size]
            slot = half * count + place
            if slot == 0:
                own[...] = part
            else:
                fold(sent[slot - 1], 0, part, main)


def final_kernel(main, tail, own, *refs):
    got, out = refs[:-1], refs[-1]
    total = own[...]
    for ref in got:
        total = total + unfold(ref, 0, own.shape[0], main, tail).astype(jnp.float32)
    out[...] = total


def final_kernel(main, tail, own, *refs):
    got, out = refs[:-1], refs[-1]
    size = own.shape[0]
    total = own[:, :main]
    for ref in got:
        total = total + ref[:size, :].astype(jnp.float32)
    out[:, :main] = total
    for rows_in, rows_out, lanes_out in folds(size, main, tail):
        total = own[rows_in, main:]
        for ref in got:
            total = total + ref[rows_out, lanes_out].astype(jnp.float32)
        out[rows_in, main:] = total


def packed(
    picture_averaged_encodings,
    caption_averaged_encodings,
    picture_mapping_matrix,
    caption_mapping_matrix,
    picture_weight_perturbation,
    caption_weight_perturbation,
    sharpness_multiplier,
    offset_additive,
):
    tensor_rank = lax.axis_index("tensor")
    data_rank = lax.axis_index("dp")
    count = lax.axis_size("tensor")
    data_count = lax.axis_size("dp")
    planes = data_count // 2
    rows, width = picture_averaged_encodings.shape
    cols = picture_mapping_matrix.shape[1]
    main = cols // 128 * 128
    tail = cols - main
    share = rows // count
    size = width // data_count
    wide = -(-2 * cols // 128) * 128
    f32, bf16 = jnp.float32, jnp.bfloat16
    ranks = jnp.arange(count, dtype=jnp.int32)
    starts = (ranks ^ tensor_rank) * share
    plain = ranks * share

    blocks = call(
        functools.partial(project_kernel, share),
        [((share, 2 * cols), bf16)] * 2 + [((2 * share, 2 * cols), bf16)],
        starts,
        caption_averaged_encodings,
        caption_mapping_matrix.T,
        caption_weight_perturbation.T,
    )
    text_far = swapped(blocks[2], "tensor", 2)
    (relay,) = call(relay_kernel, [((2 * share, 2 * cols), bf16)], blocks[1], text_far)
    text_near = swapped(relay, "tensor", 1)

    (image,) = call(
        functools.partial(project_kernel, share),
        [((rows, 2 * cols), bf16)],
        plain,
        picture_averaged_encodings,
        picture_mapping_matrix.T,
        picture_weight_perturbation.T,
        after=(blocks[0],),
    )
    image_other = swapped(image, "dp", 1)
    image_far = swapped(image, "tensor", 2)
    image_far_other = swapped(image_other, "tensor", 2)

    (text,) = call(
        functools.partial(text_rows_kernel, main, tail),
        [((share, 2 * width), bf16)],
        blocks[0],
        text_far,
        text_near,
    )
    text_two = swapped(text, "dp", 4)
    text_one = swapped(text, "dp", 2)
    text_three = swapped(text_two, "dp", 2)
    texts = [text, text_one, text_two, text_three]

    block_ids = jnp.arange(data_count, dtype=jnp.int32)
    slots = ((block_ids ^ data_rank) >> 1) + planes * ((block_ids ^ data_rank) & 1)
    core = (tensor_rank & 1).astype(jnp.int32).reshape(1)
    mine, other = call(
        turn_kernel,
        [((planes * size, 2 * rows), bf16), ((planes // 2 * size, 2 * rows), bf16)],
        slots,
        core,
        picture_averaged_encodings,
        caption_averaged_encodings,
        after=(image,),
    )
    other = swapped(other, "dp", 1)
    others = (other, swapped(other, "tensor", 1))

    (near,) = call(
        stack_kernel,
        [((4 * rows, wide), bf16)],
        image,
        image_other,
        image_far,
        image_far_other,
        after=(text_one, text_two, others[0]),
    )
    far = swapped(near, "tensor", 1)
    unit, tangent, half, tangent_half, factors = call(
        functools.partial(image_rows_kernel, main, tail, count),
        [
            ((2 * rows, width), f32),
            ((2 * rows, width), f32),
            ((2 * rows, width), bf16),
            ((2 * rows, width), bf16),
            ((2, 2 * rows, 128), f32),
        ],
        near,
        far,
    )

    scalars = jnp.concatenate([sharpness_multiplier, offset_additive])
    text_half, text_tangent_half, weight, weight_rate, weight_turned, weight_rate_turned = call(
        functools.partial(weight_kernel, planes),
        [((planes * share, width), bf16)] * 2
        + [((planes * share, 2 * rows), bf16)] * 2
        + [((2 * rows, planes * share), bf16)] * 2,
        (tensor_rank * share).astype(jnp.int32).reshape(1),
        scalars,
        half,
        tangent_half,
        *texts,
        after=(others[1],),
    )
    kept, sent = call(
        functools.partial(image_block_kernel, main, tail),
        [((2 * rows, wide), f32)] * 2,
        scalars,
        unit,
        tangent,
        factors,
        text_half,
        text_tangent_half,
        weight_turned,
        weight_rate_turned,
    )
    outs = call(
        functools.partial(text_block_kernel, planes),
        [((share, width), f32)] * 2 + [((2 * share, width), bf16)],
        scalars,
        half,
        tangent_half,
        weight,
        weight_rate,
        *texts,
        after=(kept,),
    )

    near = (tensor_rank // 2).astype(jnp.int32).reshape(1)
    tall = folded_rows(rows, main, tail)
    more = folded_rows(2 * share, main, tail)
    total, to_x, to_y, to_both = call(
        functools.partial(image_pair_kernel, main, tail, share),
        [((rows, cols), f32), ((tall + more, main), bf16)] + [((tall, main), bf16)] * 2,
        near,
        kept,
        swapped(sent, "tensor", 1),
        after=(outs[0],),
    )
    flat = [(source, source ^ (count + 2)) for source in range(data_count * count)]
    (image_back,) = call(
        functools.partial(image_sum_kernel, main, tail, share),
        [((tall, main), bf16)],
        near,
        total,
        swapped(to_x, "tensor", 2),
        swapped(to_y, "dp", 1),
        lax.ppermute(to_both, ("dp", "tensor"), flat),
    )
    image_back_other = swapped(image_back, "dp", 1)

    text_total, text_sent = call(
        forward_kernel,
        [((share, width), f32), ((share, width), bf16)],
        outs[0],
        outs[1],
        swapped(outs[2], "dp", 2),
    )
    blocks = call(
        functools.partial(text_sum_kernel, main, tail),
        [((share, cols), bf16)] * count,
        text_total,
        swapped(text_sent, "dp", 4),
        after=(image_back,),
    )
    got = [blocks[0]] + [swapped(blocks[k], "tensor", k) for k in range(1, count)]
    (text_back,) = call(fold_kernel, [((tall, main), bf16)], *got)
    text_back_other = swapped(text_back, "dp", 1)


    def head(which, order, back, back_other):
        products = call(
            functools.partial(head_kernel, main, tail, which),
            [((size, cols), f32)]
            + [((folded_rows(size, main, tail), main), bf16)] * (planes - 1),
            core,
            order,
            mine,
            *others,
            back,
            back_other,
            scratch=[((2, rows, cols), bf16)],
        )
        got = [swapped(products[k], "dp", 2 * k) for k in range(1, planes)]
        (out,) = call(
            functools.partial(final_kernel, main, tail), [((size, cols), f32)], products[0], *got
        )
        return out

    return (
        head(0, plain, image_back, image_back_other),
        head(1, starts, text_back, text_back_other),
    )


def fits(mesh):
    return mesh.shape["tensor"] == 4 and mesh.shape["dp"] == 8


def solution(mesh):
    in_specs = (
        P("dp", None),
        P("dp", None),
        P(None, "tensor"),
        P(None, "tensor"),
        P(None, "tensor"),
        P(None, "tensor"),
        P(),
        P(),
    )
    out_specs = (P("dp", "tensor"), P("dp", "tensor"))
    local = packed if fits(mesh) else general
    return jax.shard_map(local, mesh=mesh, in_specs=in_specs, out_specs=out_specs, check_vma=False)
```

profile of v0, /device:TPU:0, one launch (start us, length us, event | category | flops | bytes accessed | tf_op | source)
XLA Modules:
  0.0 92.6 jit_solution(9186142403336819583)
XLA Ops:
  3.9 1.2 %shard_map.95 = (bf16[48,576]{1,0:T(8,128)(2,1)S(1)}, bf16[48,576]{1,0:T(8,128)(2,1)S(1)}, bf16[96,576]{1,0:T(8,128)(2,1)S(1)}) custom-call(s32[4]{0:T(128)S(1)} %xor_multiply_fusion.refs_0_.refs_1_, bf16[192,1152]{1,0:T(8,128)(2,1)S(1)} %copy-done.1, bf16[288,1152]{1,0:T(8,128)(2,1)S(1)} %bitcast.7, bf16[288,1152]{1,0:T(8,128)(2,1)S(1)} %bitcast.8), custom_call_target="tpu_custom_call" | custom-call | tf_op jit(solution)/shard_map/pallas_call | solution.py:213
  5.1 3.0 %collective-permute-start.5 = (bf16[96,576]{1,0:T(8,128)(2,1)S(1)}, bf16[96,576]{1,0:T(8,128)(2,1)S(1)}, u32[]{:S(2)}, u32[]{:S(2)}) collective-permute-start(bf16[96,576]{1,0:T(8,128)(2,1)S(1)} %get-tuple-element.44), channel_id=1, source_target_pairs={{0,2},{1,3},{2,0},{3,1},{4,6},{5,7},{6,4},{7,5},{8,10},{9,11},{10,... | collective-permute-start | bytes 331784 | tf_op jit(solution)/shard_map/ppermute | solution.py:15
  9.2 1.2 %shard_map.96.refs_4_.refs_0_ = bf16[192,576]{1,0:T(8,128)(2,1)S(1)} custom-call(s32[4]{0:T(128)S(1)} %iota_multiply_fusion.refs_0_.refs_1_, bf16[192,1152]{1,0:T(8,128)(2,1)S(1)} %copy-done, bf16[288,1152]{1,0:T(8,128)(2,1)S(1)} %bitcast.9, bf16[288,1152]{1,0:T(8,128)(2,1)S(1)} %bitcast.10, bf16[48,576]{1,0:T(8,128)(2,1)S(1)} %get-tuple-element.41.refs_4_.refs_0_), custom_call_target="tpu_custom_call" | custom-call | tf_op jit(solution)/shard_map/pallas_call | solution.py:213
  10.4 1.6 %collective-permute-start.2 = (bf16[192,576]{1,0:T(8,128)(2,1)S(1)}, bf16[192,576]{1,0:T(8,128)(2,1)S(1)}, u32[]{:S(2)}, u32[]{:S(2)}) collective-permute-start(bf16[192,576]{1,0:T(8,128)(2,1)S(1)} %shard_map.96.refs_4_.refs_0_), channel_id=1, source_target_pairs={{0,4},{4,0},{8,12},{12,8},{16,20},{20,16},{24,28},{28,24},{1,5},{5... | collective-permute-start | bytes 663560 | tf_op jit(solution)/shard_map/ppermute | solution.py:15
  12.7 2.1 %shard_map.97 = (bf16[576,384]{1,0:T(8,128)(2,1)S(1)}, bf16[288,384]{1,0:T(8,128)(2,1)S(1)}) custom-call(s32[8]{0:T(128)S(1)} %multiply_add_fusion.refs_0_, s32[1]{0:T(128)} %bitcast.refs_1_.refs_0_, bf16[192,1152]{1,0:T(8,128)(2,1)S(1)} %copy-done, bf16[192,1152]{1,0:T(8,128)(2,1)S(1)} %copy-done.2, bf16[192,576]{1,0:T(8,128)(2,1)S(1)} %shard_map.96.refs_4_.refs_0_), custom_call_target="tpu_custom_call" | custom-call | tf_op jit(solution)/shard_map/pallas_call | solution.py:213
  15.6 2.6 %collective-permute-start.8 = (bf16[48,2304]{1,0:T(8,128)(2,1)S(1)}, bf16[48,2304]{1,0:T(8,128)(2,1)S(1)}, u32[]{:S(2)}, u32[]{:S(2)}) collective-permute-start(bf16[48,2304]{1,0:T(8,128)(2,1)S(1)} %shard_map.99.refs_4_.refs_5_), channel_id=1, source_target_pairs={{0,16},{4,20},{8,24},{12,28},{16,0},{20,4},{24,8},{28,12},{1,17},{... | collective-permute-start | bytes 663560 | tf_op jit(solution)/shard_map/ppermute | solution.py:15
  18.3 1.6 %collective-permute-start.7 = (bf16[48,2304]{1,0:T(8,128)(2,1)S(1)}, bf16[48,2304]{1,0:T(8,128)(2,1)S(1)}, u32[]{:S(2)}, u32[]{:S(2)}) collective-permute-start(bf16[48,2304]{1,0:T(8,128)(2,1)S(1)} %shard_map.99.refs_4_.refs_5_), channel_id=1, source_target_pairs={{0,8},{4,12},{8,0},{12,4},{16,24},{20,28},{24,16},{28,20},{1,9},{5... | collective-permute-start | bytes 663560 | tf_op jit(solution)/shard_map/ppermute | solution.py:15
  19.8 1.5 %collective-permute-start.4 = (bf16[192,576]{1,0:T(8,128)(2,1)S(1)}, bf16[192,576]{1,0:T(8,128)(2,1)S(1)}, u32[]{:S(2)}, u32[]{:S(2)}) collective-permute-start(bf16[192,576]{1,0:T(8,128)(2,1)S(1)} %collective-permute-done.2.refs_1_), channel_id=1, source_target_pairs={{0,2},{1,3},{2,0},{3,1},{4,6},{5,7},{6,4},{7,5},{8,10},{9,11},{10,... | collective-permute-start | bytes 663560 | tf_op jit(solution)/shard_map/ppermute | solution.py:15
  21.3 1.3 %collective-permute-done.refs_6_.refs_3_ = bf16[288,384]{1,0:T(8,128)(2,1)S(1)} collective-permute-done((bf16[288,384]{1,0:T(8,128)(2,1)S(1)}, bf16[288,384]{1,0:T(8,128)(2,1)S(1)}, u32[]{:S(2)}, u32[]{:S(2)}) %collective-permute-start) | collective-permute-done | bytes 221216 | tf_op jit(solution)/shard_map/ppermute | solution.py:15
  22.6 6.3 %collective-permute-done.8.refs_5_.refs_6_.refs_7_ = bf16[48,2304]{1,0:T(8,128)(2,1)S(1)} collective-permute-done((bf16[48,2304]{1,0:T(8,128)(2,1)S(1)}, bf16[48,2304]{1,0:T(8,128)(2,1)S(1)}, u32[]{:S(2)}, u32[]{:S(2)}) %collective-permute-start.8) | collective-permute-done | bytes 221216 | tf_op jit(solution)/shard_map/ppermute | solution.py:15
  29.8 1.4 %collective-permute-start.10 = (bf16[48,2304]{1,0:T(8,128)(2,1)S(1)}, bf16[48,2304]{1,0:T(8,128)(2,1)}, u32[]{:S(2)}, u32[]{:S(2)}) collective-permute-start(bf16[48,2304]{1,0:T(8,128)(2,1)S(1)} %collective-permute-done.8.refs_5_.refs_6_.refs_7_), channel_id=1, source_target_pairs={{0,8},{4,12},{8,0},{12,4},{16,24},{20,28},{24,16},{28,20},{1,9},{5... | collective-permute-start | bytes 663560 | tf_op jit(solution)/shard_map/ppermute | solution.py:15
  32.6 3.0 %shard_map.101 = (f32[384,1152]{1,0:T(8,128)S(1)}, f32[384,1152]{1,0:T(8,128)}, bf16[384,1152]{1,0:T(8,128)(2,1)S(1)}, bf16[384,1152]{1,0:T(8,128)(2,1)S(1)}, f32[2,384,128]{2,1,0:T(8,128)S(1)}) custom-call(bf16[768,640]{1,0:T(8,128)(2,1)S(1)} %shard_map.100.refs_0_, bf16[768,640]{1,0:T(8,128)(2,1)S(1)} %collective-permute-done.9.refs_1_), custom_call_target="tpu_custom_call" | custom-call | tf_op jit(solution)/shard_map/pallas_call | solution.py:213
  35.6 1.7 %collective-permute-done.10.refs_7_.refs_8_ = bf16[48,2304]{1,0:T(8,128)(2,1)} collective-permute-done((bf16[48,2304]{1,0:T(8,128)(2,1)S(1)}, bf16[48,2304]{1,0:T(8,128)(2,1)}, u32[]{:S(2)}, u32[]{:S(2)}) %collective-permute-start.10) | collective-permute-done | bytes 221216 | tf_op jit(solution)/shard_map/ppermute | solution.py:15
  37.3 2.4 %shard_map.102 = (bf16[192,1152]{1,0:T(8,128)(2,1)S(1)}, bf16[192,1152]{1,0:T(8,128)(2,1)S(1)}, bf16[192,384]{1,0:T(8,128)(2,1)S(1)}, bf16[192,384]{1,0:T(8,128)...) custom-call(s32[1]{0:T(128)} %bitcast.6.refs_0_, f32[2]{0:T(128)S(1)} %pad_maximum_fusion.refs_1_.refs_0_, ...), custom_call_target="tpu_custom_call" | custom-call | tf_op jit(solution)/shard_map/pallas_call | solution.py:213
  39.7 4.3 %shard_map.103 = (f32[384,640]{1,0:T(8,128)S(1)}, f32[384,640]{1,0:T(8,128)}) custom-call(f32[2]{0:T(128)S(1)} %pad_maximum_fusion.refs_1_.refs_0_, f32[384,1152]{1,0:T(8,128)S(1)} %get-tuple-element.46.refs_1_, f32[384,1152]{1,0:T(8,128)} %get-tuple-element.47.refs_2_, f32[2,384,128]{2,1,0:T(8,128)S(1)} %get-tuple-element.48.refs_3_, ...), custom_call_target="tpu_custom_call" | custom-call | tf_op jit(solution)/shard_map/pallas_call | solution.py:213
  44.0 3.0 %shard_map.104 = (f32[48,1152]{1,0:T(8,128)S(1)}, f32[48,1152]{1,0:T(8,128)S(1)}, bf16[96,1152]{1,0:T(8,128)(2,1)}) custom-call(f32[2]{0:T(128)S(1)} %pad_maximum_fusion.refs_1_.refs_0_, bf16[384,1152]{1,0:T(8,128)(2,1)S(1)} %get-tuple-element.49.refs_2_.refs_1_, bf16[384,1152]{1,0:T(8,128)(2,1)S(1)} %get-tuple-element.50.refs_3_.refs_2_, ...), custom_call_target="tpu_custom_call" | custom-call | tf_op jit(solution)/shard_map/pallas_call | solution.py:213
  48.4 1.4 %collective-permute-start.19 = (bf16[96,1152]{1,0:T(8,128)(2,1)}, bf16[96,1152]{1,0:T(8,128)(2,1)}, u32[]{:S(2)}, u32[]{:S(2)}) collective-permute-start(bf16[96,1152]{1,0:T(8,128)(2,1)} %get-tuple-element.69), channel_id=1, source_target_pairs={{0,8},{4,12},{8,0},{12,4},{16,24},{20,28},{24,16},{28,20},{1,9},{5... | collective-permute-start | bytes 663560 | tf_op jit(solution)/shard_map/ppermute | solution.py:15
  51.0 1.6 %collective-permute-start.12 = (bf16[336,256]{1,0:T(8,128)(2,1)S(1)}, bf16[336,256]{1,0:T(8,128)(2,1)S(1)}, u32[]{:S(2)}, u32[]{:S(2)}) collective-permute-start(bf16[336,256]{1,0:T(8,128)(2,1)S(1)} %get-tuple-element.61), channel_id=1, source_target_pairs={{0,2},{1,3},{2,0},{3,1},{4,6},{5,7},{6,4},{7,5},{8,10},{9,11},{10,... | collective-permute-start | bytes 516104 | tf_op jit(solution)/shard_map/ppermute | solution.py:15
  52.5 1.4 %collective-permute-start.13 = (bf16[224,256]{1,0:T(8,128)(2,1)S(1)}, bf16[224,256]{1,0:T(8,128)(2,1)S(1)}, u32[]{:S(2)}, u32[]{:S(2)}) collective-permute-start(bf16[224,256]{1,0:T(8,128)(2,1)S(1)} %get-tuple-element.62), channel_id=1, source_target_pairs={{0,4},{4,0},{8,12},{12,8},{16,20},{20,16},{24,28},{28,24},{1,5},{5... | collective-permute-start | bytes 344072 | tf_op jit(solution)/shard_map/ppermute | solution.py:15
  54.5 2.0 %collective-permute-done.19.refs_2_ = bf16[96,1152]{1,0:T(8,128)(2,1)} collective-permute-done((bf16[96,1152]{1,0:T(8,128)(2,1)}, bf16[96,1152]{1,0:T(8,128)(2,1)}, u32[]{:S(2)}, u32[]{:S(2)}) %collective-permute-start.19) | collective-permute-done | bytes 221216 | tf_op jit(solution)/shard_map/ppermute | solution.py:15
  57.5 2.1 %collective-permute-start.20 = (bf16[48,1152]{1,0:T(8,128)(2,1)S(1)}, bf16[48,1152]{1,0:T(8,128)(2,1)S(1)}, u32[]{:S(2)}, u32[]{:S(2)}) collective-permute-start(bf16[48,1152]{1,0:T(8,128)(2,1)S(1)} %get-tuple-element.71), channel_id=1, source_target_pairs={{0,16},{4,20},{8,24},{12,28},{16,0},{20,4},{24,8},{28,12},{1,17},{... | collective-permute-start | bytes 331784 | tf_op jit(solution)/shard_map/ppermute | solution.py:15
  59.6 1.2 %collective-permute-done.14.refs_4_ = bf16[224,256]{1,0:T(8,128)(2,1)S(1)} collective-permute-done((bf16[224,256]{1,0:T(8,128)(2,1)S(1)}, bf16[224,256]{1,0:T(8,128)(2,1)S(1)}, u32[]{:S(2)}, u32[]{:S(2)}) %collective-permute-start.14) | collective-permute-done | bytes 114720 | tf_op jit(solution)/shard_map/ppermute | solution.py:727
  61.7 3.8 %collective-permute-done.20.refs_1_ = bf16[48,1152]{1,0:T(8,128)(2,1)S(1)} collective-permute-done((bf16[48,1152]{1,0:T(8,128)(2,1)S(1)}, bf16[48,1152]{1,0:T(8,128)(2,1)S(1)}, u32[]{:S(2)}, u32[]{:S(2)}) %collective-permute-start.20) | collective-permute-done | bytes 110624 | tf_op jit(solution)/shard_map/ppermute | solution.py:15
  65.7 1.6 %collective-permute-start.22 = (bf16[48,288]{1,0:T(8,128)(2,1)S(1)}, bf16[48,288]{1,0:T(8,128)(2,1)S(1)}, u32[]{:S(2)}, u32[]{:S(2)}) collective-permute-start(bf16[48,288]{1,0:T(8,128)(2,1)S(1)} %get-tuple-element.74), channel_id=1, source_target_pairs={{0,2},{1,3},{2,0},{3,1},{4,6},{5,7},{6,4},{7,5},{8,10},{9,11},{10,... | collective-permute-start | bytes 82952 | tf_op jit(solution)/shard_map/ppermute | solution.py:15
  67.6 2.2 %collective-permute-done.22.refs_2_ = bf16[48,288]{1,0:T(8,128)(2,1)S(1)} collective-permute-done((bf16[48,288]{1,0:T(8,128)(2,1)S(1)}, bf16[48,288]{1,0:T(8,128)(2,1)S(1)}, u32[]{:S(2)}, u32[]{:S(2)}) %collective-permute-start.22) | collective-permute-done | bytes 27680 | tf_op jit(solution)/shard_map/ppermute | solution.py:15
  70.8 1.4 %collective-permute-start.24 = (bf16[224,256]{1,0:T(8,128)(2,1)S(1)}, bf16[224,256]{1,0:T(8,128)(2,1)S(1)}, u32[]{:S(2)}, u32[]{:S(2)}) collective-permute-start(bf16[224,256]{1,0:T(8,128)(2,1)S(1)} %shard_map.111.refs_5_), channel_id=1, source_target_pairs={{0,4},{4,0},{8,12},{12,8},{16,20},{20,16},{24,28},{28,24},{1,5},{5... | collective-permute-start | bytes 344072 | tf_op jit(solution)/shard_map/ppermute | solution.py:15
  72.2 1.2 %shard_map.107 = (f32[144,288]{1,0:T(8,128)S(1)}, bf16[176,256]{1,0:T(8,128)(2,1)S(1)}, bf16[176,256]{1,0:T(8,128)(2,1)S(1)}, bf16[176,256]{1,0:T(8,128)(2,1)S(1)}) custom-call(s32[1]{0:T(128)} %bitcast.refs_1_.refs_0_, s32[4]{0:T(128)S(1)} %iota_multiply_fusion.refs_0_.refs_1_, bf16[576,384]{1,0:T(8,128)(2,1)S(1)} %get-tuple-element.42.refs_2_, ...), custom_call_target="tpu_custom_call" | custom-call | tf_op jit(solution)/shard_map/pallas_call | solution.py:213
  73.6 3.4 %collective-permute-start.17 = (bf16[176,256]{1,0:T(8,128)(2,1)S(1)}, bf16[176,256]{1,0:T(8,128)(2,1)S(1)}, u32[]{:S(2)}, u32[]{:S(2)}) collective-permute-start(bf16[176,256]{1,0:T(8,128)(2,1)S(1)} %get-tuple-element.66), channel_id=1, source_target_pairs={{0,16},{4,20},{8,24},{12,28},{16,0},{20,4},{24,8},{28,12},{1,17},{... | collective-permute-start | bytes 270344 | tf_op jit(solution)/shard_map/ppermute | solution.py:15
  77.8 1.2 %shard_map.112 = (f32[144,288]{1,0:T(8,128)S(1)}, bf16[176,256]{1,0:T(8,128)(2,1)S(1)}, bf16[176,256]{1,0:T(8,128)(2,1)S(1)}, bf16[176,256]{1,0:T(8,128)(2,1)S(1)}) custom-call(s32[1]{0:T(128)} %bitcast.refs_1_.refs_0_, s32[4]{0:T(128)S(1)} %xor_multiply_fusion.refs_0_.refs_1_, bf16[576,384]{1,0:T(8,128)(2,1)S(1)} %get-tuple-element.42.refs_2_, ...), custom_call_target="tpu_custom_call" | custom-call | tf_op jit(solution)/shard_map/pallas_call | solution.py:213
  79.1 3.5 %collective-permute-start.26 = (bf16[176,256]{1,0:T(8,128)(2,1)S(1)}, bf16[176,256]{1,0:T(8,128)(2,1)S(1)}, u32[]{:S(2)}, u32[]{:S(2)}) collective-permute-start(bf16[176,256]{1,0:T(8,128)(2,1)S(1)} %get-tuple-element.78), channel_id=1, source_target_pairs={{0,16},{4,20},{8,24},{12,28},{16,0},{20,4},{24,8},{28,12},{1,17},{... | collective-permute-start | bytes 270344 | tf_op jit(solution)/shard_map/ppermute | solution.py:15
  83.5 1.2 %collective-permute-done.17.refs_2_ = bf16[176,256]{1,0:T(8,128)(2,1)S(1)} collective-permute-done((bf16[176,256]{1,0:T(8,128)(2,1)S(1)}, bf16[176,256]{1,0:T(8,128)(2,1)S(1)}, u32[]{:S(2)}, u32[]{:S(2)}) %collective-permute-start.17) | collective-permute-done | bytes 90144 | tf_op jit(solution)/shard_map/ppermute | solution.py:15
  85.4 6.4 %collective-permute-done.26.refs_2_ = bf16[176,256]{1,0:T(8,128)(2,1)S(1)} collective-permute-done((bf16[176,256]{1,0:T(8,128)(2,1)S(1)}, bf16[176,256]{1,0:T(8,128)(2,1)S(1)}, u32[]{:S(2)}, u32[]{:S(2)}) %collective-permute-start.26) | collective-permute-done | bytes 90144 | tf_op jit(solution)/shard_map/ppermute | solution.py:15
  (69 shorter events, 16.9 us)
Async XLA Ops:
  0.6 7.5 %copy-start = (bf16[192,1152]{1,0:T(8,128)(2,1)S(1)}, bf16[192,1152]{1,0:T(8,128)(2,1)}, u32[]{:S(2)}) copy-start(bf16[192,1152]{1,0:T(8,128)(2,1)} %refs_2_.1) | copy-start | bytes 1327108
  3.9 4.2 %copy-start.7 = (bf16[1152,288]{0,1:T(8,128)(2,1)S(1)}, bf16[1152,288]{0,1:T(8,128)(2,1)}, u32[]{:S(2)}) copy-start(bf16[1152,288]{0,1:T(8,128)(2,1)} %param.10) | copy-start | bytes 1990660
  3.9 8.7 %copy-start.2 = (bf16[192,1152]{1,0:T(8,128)(2,1)S(1)}, bf16[192,1152]{1,0:T(8,128)(2,1)}, u32[]{:S(2)}) copy-start(bf16[192,1152]{1,0:T(8,128)(2,1)} %refs_3_.1) | copy-start | bytes 1327108
  5.1 7.4 %collective-permute-start.5 = (bf16[96,576]{1,0:T(8,128)(2,1)S(1)}, bf16[96,576]{1,0:T(8,128)(2,1)S(1)}, u32[]{:S(2)}, u32[]{:S(2)}) collective-permute-start(bf16[96,576]{1,0:T(8,128)(2,1)S(1)} %get-tuple-element.44), channel_id=1, source_target_pairs={{0,2},{1,3},{2,0},{3,1},{4,6},{5,7},{6,4},{7,5},{8,10},{9,11},{10,... | collective-permute-start | bytes 331784 | tf_op jit(solution)/shard_map/ppermute | solution.py:15
  10.4 9.4 %collective-permute-start.2 = (bf16[192,576]{1,0:T(8,128)(2,1)S(1)}, bf16[192,576]{1,0:T(8,128)(2,1)S(1)}, u32[]{:S(2)}, u32[]{:S(2)}) collective-permute-start(bf16[192,576]{1,0:T(8,128)(2,1)S(1)} %shard_map.96.refs_4_.refs_0_), channel_id=1, source_target_pairs={{0,4},{4,0},{8,12},{12,8},{16,20},{20,16},{24,28},{28,24},{1,5},{5... | collective-permute-start | bytes 663560 | tf_op jit(solution)/shard_map/ppermute | solution.py:15
  12.0 9.3 %collective-permute-start.3 = (bf16[192,576]{1,0:T(8,128)(2,1)S(1)}, bf16[192,576]{1,0:T(8,128)(2,1)S(1)}, u32[]{:S(2)}, u32[]{:S(2)}) collective-permute-start(bf16[192,576]{1,0:T(8,128)(2,1)S(1)} %shard_map.96.refs_4_.refs_0_), channel_id=1, source_target_pairs={{0,2},{1,3},{2,0},{3,1},{4,6},{5,7},{6,4},{7,5},{8,10},{9,11},{10,... | collective-permute-start | bytes 663560 | tf_op jit(solution)/shard_map/ppermute | solution.py:15
  12.6 2.9 %collective-permute-start.6 = (bf16[96,576]{1,0:T(8,128)(2,1)S(1)}, bf16[96,576]{1,0:T(8,128)(2,1)S(1)}, u32[]{:S(2)}, u32[]{:S(2)}) collective-permute-start(bf16[96,576]{1,0:T(8,128)(2,1)S(1)} %shard_map.98), channel_id=1, source_target_pairs={{0,1},{1,0},{2,3},{3,2},{4,5},{5,4},{6,7},{7,6},{8,9},{9,8},{10,11... | collective-permute-start | bytes 331784 | tf_op jit(solution)/shard_map/ppermute | solution.py:15
  14.8 7.9 %collective-permute-start = (bf16[288,384]{1,0:T(8,128)(2,1)S(1)}, bf16[288,384]{1,0:T(8,128)(2,1)S(1)}, u32[]{:S(2)}, u32[]{:S(2)}) collective-permute-start(bf16[288,384]{1,0:T(8,128)(2,1)S(1)} %get-tuple-element.43), channel_id=1, source_target_pairs={{0,4},{4,0},{8,12},{12,8},{16,20},{20,16},{24,28},{28,24},{1,5},{5... | collective-permute-start | bytes 663560 | tf_op jit(solution)/shard_map/ppermute | solution.py:15
  15.6 13.3 %collective-permute-start.8 = (bf16[48,2304]{1,0:T(8,128)(2,1)S(1)}, bf16[48,2304]{1,0:T(8,128)(2,1)S(1)}, u32[]{:S(2)}, u32[]{:S(2)}) collective-permute-start(bf16[48,2304]{1,0:T(8,128)(2,1)S(1)} %shard_map.99.refs_4_.refs_5_), channel_id=1, source_target_pairs={{0,16},{4,20},{8,24},{12,28},{16,0},{20,4},{24,8},{28,12},{1,17},{... | collective-permute-start | bytes 663560 | tf_op jit(solution)/shard_map/ppermute | solution.py:15
  18.3 10.9 %collective-permute-start.7 = (bf16[48,2304]{1,0:T(8,128)(2,1)S(1)}, bf16[48,2304]{1,0:T(8,128)(2,1)S(1)}, u32[]{:S(2)}, u32[]{:S(2)}) collective-permute-start(bf16[48,2304]{1,0:T(8,128)(2,1)S(1)} %shard_map.99.refs_4_.refs_5_), channel_id=1, source_target_pairs={{0,8},{4,12},{8,0},{12,4},{16,24},{20,28},{24,16},{28,20},{1,9},{5... | collective-permute-start | bytes 663560 | tf_op jit(solution)/shard_map/ppermute | solution.py:15
  19.8 9.3 %collective-permute-start.4 = (bf16[192,576]{1,0:T(8,128)(2,1)S(1)}, bf16[192,576]{1,0:T(8,128)(2,1)S(1)}, u32[]{:S(2)}, u32[]{:S(2)}) collective-permute-start(bf16[192,576]{1,0:T(8,128)(2,1)S(1)} %collective-permute-done.2.refs_1_), channel_id=1, source_target_pairs={{0,2},{1,3},{2,0},{3,1},{4,6},{5,7},{6,4},{7,5},{8,10},{9,11},{10,... | collective-permute-start | bytes 663560 | tf_op jit(solution)/shard_map/ppermute | solution.py:15
  29.2 3.4 %collective-permute-start.9 = (bf16[768,640]{1,0:T(8,128)(2,1)S(1)}, bf16[768,640]{1,0:T(8,128)(2,1)S(1)}, u32[]{:S(2)}, u32[]{:S(2)}) collective-permute-start(bf16[768,640]{1,0:T(8,128)(2,1)S(1)} %shard_map.100.refs_0_), channel_id=1, source_target_pairs={{0,1},{1,0},{2,3},{3,2},{4,5},{5,4},{6,7},{7,6},{8,9},{9,8},{10,11... | collective-permute-start | bytes 2949128 | tf_op jit(solution)/shard_map/ppermute | solution.py:15
  29.3 6.3 %collective-permute-start.1 = (bf16[288,384]{1,0:T(8,128)(2,1)S(1)}, bf16[288,384]{1,0:T(8,128)(2,1)S(1)}, u32[]{:S(2)}, u32[]{:S(2)}) collective-permute-start(bf16[288,384]{1,0:T(8,128)(2,1)S(1)} %collective-permute-done.refs_6_.refs_3_), channel_id=1, source_target_pairs={{0,1},{1,0},{2,3},{3,2},{4,5},{5,4},{6,7},{7,6},{8,9},{9,8},{10,11... | collective-permute-start | bytes 663560 | tf_op jit(solution)/shard_map/ppermute | solution.py:15
  29.8 7.5 %collective-permute-start.10 = (bf16[48,2304]{1,0:T(8,128)(2,1)S(1)}, bf16[48,2304]{1,0:T(8,128)(2,1)}, u32[]{:S(2)}, u32[]{:S(2)}) collective-permute-start(bf16[48,2304]{1,0:T(8,128)(2,1)S(1)} %collective-permute-done.8.refs_5_.refs_6_.refs_7_), channel_id=1, source_target_pairs={{0,8},{4,12},{8,0},{12,4},{16,24},{20,28},{24,16},{28,20},{1,9},{5... | collective-permute-start | bytes 663560 | tf_op jit(solution)/shard_map/ppermute | solution.py:15
  44.0 5.8 %collective-permute-start.11 = (f32[384,640]{1,0:T(8,128)}, f32[384,640]{1,0:T(8,128)S(1)}, u32[]{:S(2)}, u32[]{:S(2)}) collective-permute-start(f32[384,640]{1,0:T(8,128)} %get-tuple-element.56), channel_id=1, source_target_pairs={{0,1},{1,0},{2,3},{3,2},{4,5},{5,4},{6,7},{7,6},{8,9},{9,8},{10,11... | collective-permute-start | bytes 2949128 | tf_op jit(solution)/shard_map/ppermute | solution.py:15
  48.4 8.2 %collective-permute-start.19 = (bf16[96,1152]{1,0:T(8,128)(2,1)}, bf16[96,1152]{1,0:T(8,128)(2,1)}, u32[]{:S(2)}, u32[]{:S(2)}) collective-permute-start(bf16[96,1152]{1,0:T(8,128)(2,1)} %get-tuple-element.69), channel_id=1, source_target_pairs={{0,8},{4,12},{8,0},{12,4},{16,24},{20,28},{24,16},{28,20},{1,9},{5... | collective-permute-start | bytes 663560 | tf_op jit(solution)/shard_map/ppermute | solution.py:15
  50.7 5.8 %copy-start.10 = (f32[48,1152]{1,0:T(8,128)S(1)}, f32[48,1152]{1,0:T(8,128)}, u32[]{:S(2)}) copy-start(f32[48,1152]{1,0:T(8,128)} %copy-done.9) | copy-start | bytes 663556
  51.0 9.8 %collective-permute-start.12 = (bf16[336,256]{1,0:T(8,128)(2,1)S(1)}, bf16[336,256]{1,0:T(8,128)(2,1)S(1)}, u32[]{:S(2)}, u32[]{:S(2)}) collective-permute-start(bf16[336,256]{1,0:T(8,128)(2,1)S(1)} %get-tuple-element.61), channel_id=1, source_target_pairs={{0,2},{1,3},{2,0},{3,1},{4,6},{5,7},{6,4},{7,5},{8,10},{9,11},{10,... | collective-permute-start | bytes 516104 | tf_op jit(solution)/shard_map/ppermute | solution.py:15
  52.5 7.1 %collective-permute-start.13 = (bf16[224,256]{1,0:T(8,128)(2,1)S(1)}, bf16[224,256]{1,0:T(8,128)(2,1)S(1)}, u32[]{:S(2)}, u32[]{:S(2)}) collective-permute-start(bf16[224,256]{1,0:T(8,128)(2,1)S(1)} %get-tuple-element.62), channel_id=1, source_target_pairs={{0,4},{4,0},{8,12},{12,8},{16,20},{20,16},{24,28},{28,24},{1,5},{5... | collective-permute-start | bytes 344072 | tf_op jit(solution)/shard_map/ppermute | solution.py:15
  53.9 6.9 %collective-permute-start.14 = (bf16[224,256]{1,0:T(8,128)(2,1)S(1)}, bf16[224,256]{1,0:T(8,128)(2,1)S(1)}, u32[]{:S(2)}, u32[]{:S(2)}) collective-permute-start(bf16[224,256]{1,0:T(8,128)(2,1)S(1)} %get-tuple-element.63), channel_id=1, source_target_pairs={{0,6},{1,7},{2,4},{3,5},{4,2},{5,3},{6,0},{7,1},{8,14},{9,15},{10,... | collective-permute-start | bytes 344072 | tf_op jit(solution)/shard_map/ppermute | solution.py:727
  57.5 8.0 %collective-permute-start.20 = (bf16[48,1152]{1,0:T(8,128)(2,1)S(1)}, bf16[48,1152]{1,0:T(8,128)(2,1)S(1)}, u32[]{:S(2)}, u32[]{:S(2)}) collective-permute-start(bf16[48,1152]{1,0:T(8,128)(2,1)S(1)} %get-tuple-element.71), channel_id=1, source_target_pairs={{0,16},{4,20},{8,24},{12,28},{16,0},{20,4},{24,8},{28,12},{1,17},{... | collective-permute-start | bytes 331784 | tf_op jit(solution)/shard_map/ppermute | solution.py:15
  61.0 11.2 %collective-permute-start.15 = (bf16[224,256]{1,0:T(8,128)(2,1)S(1)}, bf16[224,256]{1,0:T(8,128)(2,1)S(1)}, u32[]{:S(2)}, u32[]{:S(2)}) collective-permute-start(bf16[224,256]{1,0:T(8,128)(2,1)S(1)} %shard_map.106.refs_5_.refs_2_), channel_id=1, source_target_pairs={{0,4},{4,0},{8,12},{12,8},{16,20},{20,16},{24,28},{28,24},{1,5},{5... | collective-permute-start | bytes 344072 | tf_op jit(solution)/shard_map/ppermute | solution.py:15
  65.6 1.9 %collective-permute-start.21 = (bf16[48,288]{1,0:T(8,128)(2,1)S(1)}, bf16[48,288]{1,0:T(8,128)(2,1)S(1)}, u32[]{:S(2)}, u32[]{:S(2)}) collective-permute-start(bf16[48,288]{1,0:T(8,128)(2,1)S(1)} %get-tuple-element.73), channel_id=1, source_target_pairs={{0,1},{1,0},{2,3},{3,2},{4,5},{5,4},{6,7},{7,6},{8,9},{9,8},{10,11... | collective-permute-start | bytes 82952 | tf_op jit(solution)/shard_map/ppermute | solution.py:15
  65.7 4.0 %collective-permute-start.22 = (bf16[48,288]{1,0:T(8,128)(2,1)S(1)}, bf16[48,288]{1,0:T(8,128)(2,1)S(1)}, u32[]{:S(2)}, u32[]{:S(2)}) collective-permute-start(bf16[48,288]{1,0:T(8,128)(2,1)S(1)} %get-tuple-element.74), channel_id=1, source_target_pairs={{0,2},{1,3},{2,0},{3,1},{4,6},{5,7},{6,4},{7,5},{8,10},{9,11},{10,... | collective-permute-start | bytes 82952 | tf_op jit(solution)/shard_map/ppermute | solution.py:15
  67.3 3.4 %collective-permute-start.23 = (bf16[48,288]{1,0:T(8,128)(2,1)S(1)}, bf16[48,288]{1,0:T(8,128)(2,1)S(1)}, u32[]{:S(2)}, u32[]{:S(2)}) collective-permute-start(bf16[48,288]{1,0:T(8,128)(2,1)S(1)} %get-tuple-element.75), channel_id=1, source_target_pairs={{0,3},{1,2},{2,1},{3,0},{4,7},{5,6},{6,5},{7,4},{8,11},{9,10},{10,... | collective-permute-start | bytes 82952 | tf_op jit(solution)/shard_map/ppermute | solution.py:15
  70.8 7.0 %collective-permute-start.24 = (bf16[224,256]{1,0:T(8,128)(2,1)S(1)}, bf16[224,256]{1,0:T(8,128)(2,1)S(1)}, u32[]{:S(2)}, u32[]{:S(2)}) collective-permute-start(bf16[224,256]{1,0:T(8,128)(2,1)S(1)} %shard_map.111.refs_5_), channel_id=1, source_target_pairs={{0,4},{4,0},{8,12},{12,8},{16,20},{20,16},{24,28},{28,24},{1,5},{5... | collective-permute-start | bytes 344072 | tf_op jit(solution)/shard_map/ppermute | solution.py:15
  73.4 9.2 %collective-permute-start.16 = (bf16[176,256]{1,0:T(8,128)(2,1)S(1)}, bf16[176,256]{1,0:T(8,128)(2,1)S(1)}, u32[]{:S(2)}, u32[]{:S(2)}) collective-permute-start(bf16[176,256]{1,0:T(8,128)(2,1)S(1)} %get-tuple-element.65), channel_id=1, source_target_pairs={{0,8},{4,12},{8,0},{12,4},{16,24},{20,28},{24,16},{28,20},{1,9},{5... | collective-permute-start | bytes 270344 | tf_op jit(solution)/shard_map/ppermute | solution.py:15
  73.6 11.1 %collective-permute-start.17 = (bf16[176,256]{1,0:T(8,128)(2,1)S(1)}, bf16[176,256]{1,0:T(8,128)(2,1)S(1)}, u32[]{:S(2)}, u32[]{:S(2)}) collective-permute-start(bf16[176,256]{1,0:T(8,128)(2,1)S(1)} %get-tuple-element.66), channel_id=1, source_target_pairs={{0,16},{4,20},{8,24},{12,28},{16,0},{20,4},{24,8},{28,12},{1,17},{... | collective-permute-start | bytes 270344 | tf_op jit(solution)/shard_map/ppermute | solution.py:15
  76.9 7.7 %collective-permute-start.18 = (bf16[176,256]{1,0:T(8,128)(2,1)S(1)}, bf16[176,256]{1,0:T(8,128)(2,1)S(1)}, u32[]{:S(2)}, u32[]{:S(2)}) collective-permute-start(bf16[176,256]{1,0:T(8,128)(2,1)S(1)} %get-tuple-element.67), channel_id=1, source_target_pairs={{0,24},{4,28},{8,16},{12,20},{16,8},{20,12},{24,0},{28,4},{1,25},{... | collective-permute-start | bytes 270344 | tf_op jit(solution)/shard_map/ppermute | solution.py:15
  79.0 6.4 %collective-permute-start.25 = (bf16[176,256]{1,0:T(8,128)(2,1)S(1)}, bf16[176,256]{1,0:T(8,128)(2,1)S(1)}, u32[]{:S(2)}, u32[]{:S(2)}) collective-permute-start(bf16[176,256]{1,0:T(8,128)(2,1)S(1)} %get-tuple-element.77), channel_id=1, source_target_pairs={{0,8},{4,12},{8,0},{12,4},{16,24},{20,28},{24,16},{28,20},{1,9},{5... | collective-permute-start | bytes 270344 | tf_op jit(solution)/shard_map/ppermute | solution.py:15
  79.1 12.7 %collective-permute-start.26 = (bf16[176,256]{1,0:T(8,128)(2,1)S(1)}, bf16[176,256]{1,0:T(8,128)(2,1)S(1)}, u32[]{:S(2)}, u32[]{:S(2)}) collective-permute-start(bf16[176,256]{1,0:T(8,128)(2,1)S(1)} %get-tuple-element.78), channel_id=1, source_target_pairs={{0,16},{4,20},{8,24},{12,28},{16,0},{20,4},{24,8},{28,12},{1,17},{... | collective-permute-start | bytes 270344 | tf_op jit(solution)/shard_map/ppermute | solution.py:15
  82.6 9.3 %collective-permute-start.27 = (bf16[176,256]{1,0:T(8,128)(2,1)S(1)}, bf16[176,256]{1,0:T(8,128)(2,1)S(1)}, u32[]{:S(2)}, u32[]{:S(2)}) collective-permute-start(bf16[176,256]{1,0:T(8,128)(2,1)S(1)} %get-tuple-element.79), channel_id=1, source_target_pairs={{0,24},{4,28},{8,16},{12,20},{16,8},{20,12},{24,0},{28,4},{1,25},{... | collective-permute-start | bytes 270344 | tf_op jit(solution)/shard_map/ppermute | solution.py:15
  (7 other events, 6.7 us)
where the time goes:
time: 93 us; the launch traced here: 92.6 us
  starting transfers between devices  33.7 us (36%)
  waiting for transfers between devices  27.2 us (29%)
  Pallas kernels  22.8 us (25%)
  local copies, waits for them, and re-layouts  6.66 us (7%)
  between operations  2.11 us (2%)
    ppermute x27, starting transfers between devices, swapped(): lax.ppermute(value, axis, [(source, source ^ mask) for source in range(co...  33.1 us
    ppermute x27, waiting for transfers between devices, swapped(): lax.ppermute(value, axis, [(source, source ^ mask) for source in range(co...  26 us
    pallas_call x19, Pallas kernels, call(): pl.pallas_call(body, out_shape=[jax.ShapeDtypeStruct(shape, dtype) for sh...  22.8 us
    unnamed x22, local copies, waits for them, and re-layouts  6.66 us
  transfers between devices with their start and end apart: 28, of which 11 were waited for; matrix products, arithmetic and copies ran while one was open for 0% of the time, Pallas kernels for 15%

commit v1 on v0

--- a/solution.py
+++ b/solution.py
@@ -217,7 +217,7 @@
         + [pl.BlockSpec(memory_space=pl.ANY) for _ in after],
         out_specs=[pl.BlockSpec(memory_space=pltpu.VMEM) for _ in outs],
         scratch_shapes=[pltpu.VMEM(shape, dtype) for shape, dtype in scratch],
-        compiler_params=pltpu.CompilerParams(vmem_limit_bytes=48 * 1024 * 1024),
+        compiler_params=pltpu.CompilerParams(vmem_limit_bytes=24 * 1024 * 1024),
     )(*args, *after)
 
 
@@ -314,7 +314,7 @@
 STEP = 48
 
 
-def image_rows_kernel(main, tail, count, near, far, unit, tangent, half, tangent_half, factors):
+def image_rows_kernel(main, tail, count, near, far, unit, tangent, half_both, factors):
     rows = unit.shape[0] // 2
     for shard in range(2):
         held = [
@@ -332,8 +332,9 @@
             one, two = unit_rows(values, rates, inverse, rate)
             unit[there, :] = one
             tangent[there, :] = two
-            half[there, :] = one.astype(jnp.bfloat16)
-            tangent_half[there, :] = two.astype(jnp.bfloat16)
+            half_both[there, :] = one.astype(jnp.bfloat16)
+            below = pl.ds(pl.multiple_of((2 + shard) * rows + step * STEP, STEP), STEP)
+            half_both[below, :] = two.astype(jnp.bfloat16)
             factors[0, there, :] = jnp.broadcast_to(inverse, (STEP, 128))
             factors[1, there, :] = jnp.broadcast_to(rate, (STEP, 128))
 
@@ -345,21 +346,21 @@
     return unit_rows(values, rates, inverse, rate) + (inverse, rate)
 
 
-def weight_kernel(slots, start, scalars, half, tangent_half, *refs):
-    texts, outs = refs[:slots], refs[slots:]
-    text_half, text_tangent_half, weight, weight_rate, weight_turned, weight_rate_turned = outs
+def weight_kernel(slots, start, scalars, half_both, *refs):
+    texts, (text_both, weights, weights_turned) = refs[:slots], refs[slots:]
     bf16 = jnp.bfloat16
     share = texts[0].shape[0]
+    count, images = slots * share, half_both.shape[0] // 2
     multiplier, bias = scalars[0], scalars[1]
     for slot, text in enumerate(texts):
-        here = slice(slot * share, (slot + 1) * share)
         unit, tangent, _, _ = text_rows(text)
-        text_half[here, :] = unit.astype(bf16)
-        text_tangent_half[here, :] = tangent.astype(bf16)
-    logits = multiplier * matmul_nt(text_half[...], half[...]) + bias
+        text_both[slot * share : (slot + 1) * share, :] = unit.astype(bf16)
+        text_both[count + slot * share : count + (slot + 1) * share, :] = tangent.astype(bf16)
+    half, tangent_half = half_both[:images, :], half_both[images:, :]
+    text_half, text_tangent_half = text_both[:count, :], text_both[count:, :]
+    logits = multiplier * matmul_nt(text_half, half) + bias
     logit_rate = multiplier * (
-        matmul_nt(text_half[...], tangent_half[...])
-        + matmul_nt(text_tangent_half[...], half[...])
+        matmul_nt(text_half, tangent_half) + matmul_nt(text_tangent_half, half)
     )
     probability = jax.nn.sigmoid(logits)
     text_ids = lax.broadcasted_iota(jnp.int32, logits.shape, 0)
@@ -367,23 +368,20 @@
     positive = jnp.where((text_ids < share) & (text_ids + start[0] == image_ids), 1.0, 0.0)
     value = probability - positive
     value_rate = probability * (1.0 - probability) * logit_rate
-    weight[...] = value.astype(bf16)
-    weight_rate[...] = value_rate.astype(bf16)
-    weight_turned[...] = value.T.astype(bf16)
-    weight_rate_turned[...] = value_rate.T.astype(bf16)
-
-
-def text_block_kernel(slots, scalars, half, tangent_half, weight, weight_rate, *refs):
+    weights[:, :images] = value_rate.astype(bf16)
+    weights[:, images:] = value.astype(bf16)
+    weights_turned[:, :count] = value_rate.T.astype(bf16)
+    weights_turned[:, count:] = value.T.astype(bf16)
+
+
+def text_block_kernel(slots, scalars, half_both, weights, *refs):
     texts, sums = refs[:slots], refs[slots:]
-    share = texts[0].shape[0]
-    multiplier = scalars[0]
-    grad = multiplier * matmul(weight[...], half[...])
-    grad_rate = multiplier * (
-        matmul(weight_rate[...], half[...]) + matmul(weight[...], tangent_half[...])
-    )
+    share, images = texts[0].shape[0], half_both.shape[0] // 2
+    grad = matmul(weights[:, images:], half_both[:images, :])
+    grad_rate = matmul(weights[...], half_both[...])
     for slot, text in enumerate(texts):
         here = slice(slot * share, (slot + 1) * share)
-        back = back_rows(*text_rows(text), grad[here], grad_rate[here])
+        back = scalars[0] * back_rows(*text_rows(text), grad[here], grad_rate[here])
         if slot % 2 == 0:
             sums[slot // 2][...] = back
         else:
@@ -397,38 +395,16 @@
     sent[...] = (middle[...] + got[share:, :].astype(jnp.float32)).astype(jnp.bfloat16)
 
 
-def image_block_kernel(
-    main,
-    tail,
-    scalars,
-    unit,
-    tangent,
-    factors,
-    text_half,
-    text_tangent_half,
-    weight,
-    weight_rate,
-    kept,
-    sent,
-):
-    rows = unit.shape[0] // 2
-    count = 4
-    multiplier = scalars[0]
+def image_block_kernel(main, tail, scalars, unit, tangent, factors, text_both, weights, kept, sent):
+    rows, width = unit.shape[0] // 2, unit.shape[1]
+    count, texts = width // (main + tail), text_both.shape[0] // 2
+    grads = matmul(weights[:, texts:], text_both[:texts, :])
+    grad_rates = matmul(weights[...], text_both[...])
     for shard in range(2):
         here = slice(shard * rows, (shard + 1) * rows)
-        grad = multiplier * matmul(weight[here, :], text_half[...])
-        grad_rate = multiplier * (
-            matmul(weight_rate[here, :], text_half[...])
-            + matmul(weight[here, :], text_tangent_half[...])
-        )
-        back = back_rows(
-            unit[here, :],
-            tangent[here, :],
-            factors[0, here, :1],
-            factors[1, here, :1],
-            grad,
-            grad_rate,
-        )
+        inverse, rate = factors[0, here, :1], factors[1, here, :1]
+        back = back_rows(unit[here, :], tangent[here, :], inverse, rate, grads[here], grad_rates[here])
+        back = scalars[0] * back
         for k in range(count):
             out = (kept, sent)[k % 2]
             to = slice(k // 2 * rows, (k // 2 + 1) * rows)
@@ -655,13 +631,12 @@
         after=(text_one, text_two, others[0]),
     )
     far = swapped(near, "tensor", 1)
-    unit, tangent, half, tangent_half, factors = call(
+    unit, tangent, half_both, factors = call(
         functools.partial(image_rows_kernel, main, tail, count),
         [
             ((2 * rows, width), f32),
             ((2 * rows, width), f32),
-            ((2 * rows, width), bf16),
-            ((2 * rows, width), bf16),
+            ((4 * rows, width), bf16),
             ((2, 2 * rows, 128), f32),
         ],
         near,
@@ -669,15 +644,16 @@
     )
 
     scalars = jnp.concatenate([sharpness_multiplier, offset_additive])
-    text_half, text_tangent_half, weight, weight_rate, weight_turned, weight_rate_turned = call(
+    text_both, weights, weights_turned = call(
         functools.partial(weight_kernel, planes),
-        [((planes * share, width), bf16)] * 2
-        + [((planes * share, 2 * rows), bf16)] * 2
-        + [((2 * rows, planes * share), bf16)] * 2,
+        [
+            ((2 * planes * share, width), bf16),
+            ((planes * share, 4 * rows), bf16),
+            ((2 * rows, 2 * planes * share), bf16),
+        ],
         (tensor_rank * share).astype(jnp.int32).reshape(1),
         scalars,
-        half,
-        tangent_half,
+        half_both,
         *texts,
         after=(others[1],),
     )
@@ -688,19 +664,15 @@
         unit,
         tangent,
         factors,
-        text_half,
-        text_tangent_half,
-        weight_turned,
-        weight_rate_turned,
+        text_both,
+        weights_turned,
     )
     outs = call(
         functools.partial(text_block_kernel, planes),
         [((share, width), f32)] * 2 + [((2 * share, width), bf16)],
         scalars,
-        half,
-        tangent_half,
-        weight,
-        weight_rate,
+        half_both,
+        weights,
         *texts,
         after=(kept,),
     )
@@ -728,27 +700,8 @@
     )
     image_back_other = swapped(image_back, "dp", 1)
 
-    text_total, text_sent = call(
-        forward_kernel,
-        [((share, width), f32), ((share, width), bf16)],
-        outs[0],
-        outs[1],
-        swapped(outs[2], "dp", 2),
-    )
-    blocks = call(
-        functools.partial(text_sum_kernel, main, tail),
-        [((share, cols), bf16)] * count,
-        text_total,
-        swapped(text_sent, "dp", 4),
-        after=(image_back,),
-    )
-    got = [blocks[0]] + [swapped(blocks[k], "tensor", k) for k in range(1, count)]
-    (text_back,) = call(fold_kernel, [((tall, main), bf16)], *got)
-    text_back_other = swapped(text_back, "dp", 1)
-
-
     def head(which, order, back, back_other):
-        products = call(
+        return call(
             functools.partial(head_kernel, main, tail, which),
             [((size, cols), f32)]
             + [((folded_rows(size, main, tail), main), bf16)] * (planes - 1),
@@ -760,16 +713,35 @@
             back_other,
             scratch=[((2, rows, cols), bf16)],
         )
+
+    def summed(products):
         got = [swapped(products[k], "dp", 2 * k) for k in range(1, planes)]
-        (out,) = call(
+        return call(
             functools.partial(final_kernel, main, tail), [((size, cols), f32)], products[0], *got
-        )
-        return out
-
-    return (
-        head(0, plain, image_back, image_back_other),
-        head(1, starts, text_back, text_back_other),
-    )
+        )[0]
+
+    image_products = head(0, plain, image_back, image_back_other)
+
+    text_total, text_sent = call(
+        forward_kernel,
+        [((share, width), f32), ((share, width), bf16)],
+        outs[0],
+        outs[1],
+        swapped(outs[2], "dp", 2),
+    )
+    blocks = call(
+        functools.partial(text_sum_kernel, main, tail),
+        [((share, cols), bf16)] * count,
+        text_total,
+        swapped(text_sent, "dp", 4),
+        after=(image_back,),
+    )
+    got = [blocks[0]] + [swapped(blocks[k], "tensor", k) for k in range(1, count)]
+    (text_back,) = call(fold_kernel, [((tall, main), bf16)], *got, after=(image_products[0],))
+    text_back_other = swapped(text_back, "dp", 1)
+
+    text_products = head(1, starts, text_back, text_back_other)
+    return summed(image_products), summed(text_products)
 
 
 def fits(mesh):

time: 93 us -> 90.8 us (0.976)
  Pallas kernels: 22.8 us -> 20.6 us
    pallas_call x19, Pallas kernels: 22.8 us -> 20.6 us  [call(): pl.pallas_call(body, out_shape=[jax.ShapeDtypeStruct(shape, dtype) for sh...]
  transfers between devices with their start and end apart: 28 -> 28, of which waited for: 11 -> 11; matrix products, arithmetic and copies ran while one was open for 0% -> 0% of each run, Pallas kernels for 15% -> 14%
where the time goes in v1:
time: 90.8 us; the launch traced here: 90.4 us
  starting transfers between devices  33.6 us (37%)
  waiting for transfers between devices  27.3 us (30%)
  Pallas kernels  20.6 us (23%)
  local copies, waits for them, and re-layouts  6.64 us (7%)
  between operations  2.12 us (2%)
    ppermute x27, starting transfers between devices, swapped(): lax.ppermute(value, axis, [(source, source ^ mask) for source in range(co...  33 us
    ppermute x27, waiting for transfers between devices, swapped(): lax.ppermute(value, axis, [(source, source ^ mask) for source in range(co...  26.1 us
    pallas_call x19, Pallas kernels, call(): pl.pallas_call(body, out_shape=[jax.ShapeDtypeStruct(shape, dtype) for sh...  20.6 us
    unnamed x22, local copies, waits for them, and re-layouts  6.64 us
  transfers between devices with their start and end apart: 28, of which 11 were waited for; matrix products, arithmetic and copies ran while one was open for 0% of the time, Pallas kernels for 14%

profile of v1, /device:TPU:0, one launch (start us, length us, event | category | flops | bytes accessed | tf_op | source)
XLA Modules:
  0.0 90.4 jit_solution(8102445542348273642)
XLA Ops:
  1.7 1.1 %copy-done.5 = bf16[1152,288]{0,1:T(8,128)(2,1)S(1)} copy-done((bf16[1152,288]{0,1:T(8,128)(2,1)S(1)}, bf16[1152,288]{0,1:T(8,128)(2,1)}, u32[]{:S(2)}) %copy-start.5) | copy-done | bytes 663576
  3.9 1.2 %shard_map.95 = (bf16[48,576]{1,0:T(8,128)(2,1)S(1)}, bf16[48,576]{1,0:T(8,128)(2,1)S(1)}, bf16[96,576]{1,0:T(8,128)(2,1)S(1)}) custom-call(s32[4]{0:T(128)S(1)} %xor_multiply_fusion.refs_0_.refs_1_, bf16[192,1152]{1,0:T(8,128)(2,1)S(1)} %copy-done.1, bf16[288,1152]{1,0:T(8,128)(2,1)S(1)} %bitcast.7, bf16[288,1152]{1,0:T(8,128)(2,1)S(1)} %bitcast.8), custom_call_target="tpu_custom_call" | custom-call | tf_op jit(solution)/shard_map/pallas_call | solution.py:213
  5.1 3.0 %collective-permute-start.5 = (bf16[96,576]{1,0:T(8,128)(2,1)S(1)}, bf16[96,576]{1,0:T(8,128)(2,1)S(1)}, u32[]{:S(2)}, u32[]{:S(2)}) collective-permute-start(bf16[96,576]{1,0:T(8,128)(2,1)S(1)} %get-tuple-element.40), channel_id=1, source_target_pairs={{0,2},{1,3},{2,0},{3,1},{4,6},{5,7},{6,4},{7,5},{8,10},{9,11},{10,... | collective-permute-start | bytes 331784 | tf_op jit(solution)/shard_map/ppermute | solution.py:15
  9.2 1.2 %shard_map.96.refs_4_.refs_0_ = bf16[192,576]{1,0:T(8,128)(2,1)S(1)} custom-call(s32[4]{0:T(128)S(1)} %iota_multiply_fusion.refs_0_.refs_1_, bf16[192,1152]{1,0:T(8,128)(2,1)S(1)} %copy-done, bf16[288,1152]{1,0:T(8,128)(2,1)S(1)} %bitcast.9, bf16[288,1152]{1,0:T(8,128)(2,1)S(1)} %bitcast.10, bf16[48,576]{1,0:T(8,128)(2,1)S(1)} %get-tuple-element.37.refs_4_.refs_0_), custom_call_target="tpu_custom_call" | custom-call | tf_op jit(solution)/shard_map/pallas_call | solution.py:213
  10.4 1.6 %collective-permute-start.2 = (bf16[192,576]{1,0:T(8,128)(2,1)S(1)}, bf16[192,576]{1,0:T(8,128)(2,1)S(1)}, u32[]{:S(2)}, u32[]{:S(2)}) collective-permute-start(bf16[192,576]{1,0:T(8,128)(2,1)S(1)} %shard_map.96.refs_4_.refs_0_), channel_id=1, source_target_pairs={{0,4},{4,0},{8,12},{12,8},{16,20},{20,16},{24,28},{28,24},{1,5},{5... | collective-permute-start | bytes 663560 | tf_op jit(solution)/shard_map/ppermute | solution.py:15
  12.7 2.1 %shard_map.97 = (bf16[576,384]{1,0:T(8,128)(2,1)S(1)}, bf16[288,384]{1,0:T(8,128)(2,1)S(1)}) custom-call(s32[8]{0:T(128)S(1)} %multiply_add_fusion.refs_0_, s32[1]{0:T(128)} %bitcast.refs_1_.refs_0_, bf16[192,1152]{1,0:T(8,128)(2,1)S(1)} %copy-done, bf16[192,1152]{1,0:T(8,128)(2,1)S(1)} %copy-done.2, bf16[192,576]{1,0:T(8,128)(2,1)S(1)} %shard_map.96.refs_4_.refs_0_), custom_call_target="tpu_custom_call" | custom-call | tf_op jit(solution)/shard_map/pallas_call | solution.py:213
  15.6 2.6 %collective-permute-start.8 = (bf16[48,2304]{1,0:T(8,128)(2,1)S(1)}, bf16[48,2304]{1,0:T(8,128)(2,1)S(1)}, u32[]{:S(2)}, u32[]{:S(2)}) collective-permute-start(bf16[48,2304]{1,0:T(8,128)(2,1)S(1)} %shard_map.99.refs_3_), channel_id=1, source_target_pairs={{0,16},{4,20},{8,24},{12,28},{16,0},{20,4},{24,8},{28,12},{1,17},{... | collective-permute-start | bytes 663560 | tf_op jit(solution)/shard_map/ppermute | solution.py:15
  18.3 1.6 %collective-permute-start.7 = (bf16[48,2304]{1,0:T(8,128)(2,1)S(1)}, bf16[48,2304]{1,0:T(8,128)(2,1)S(1)}, u32[]{:S(2)}, u32[]{:S(2)}) collective-permute-start(bf16[48,2304]{1,0:T(8,128)(2,1)S(1)} %shard_map.99.refs_3_), channel_id=1, source_target_pairs={{0,8},{4,12},{8,0},{12,4},{16,24},{20,28},{24,16},{28,20},{1,9},{5... | collective-permute-start | bytes 663560 | tf_op jit(solution)/shard_map/ppermute | solution.py:15
  19.8 1.5 %collective-permute-start.4 = (bf16[192,576]{1,0:T(8,128)(2,1)S(1)}, bf16[192,576]{1,0:T(8,128)(2,1)S(1)}, u32[]{:S(2)}, u32[]{:S(2)}) collective-permute-start(bf16[192,576]{1,0:T(8,128)(2,1)S(1)} %collective-permute-done.2.refs_1_), channel_id=1, source_target_pairs={{0,2},{1,3},{2,0},{3,1},{4,6},{5,7},{6,4},{7,5},{8,10},{9,11},{10,... | collective-permute-start | bytes 663560 | tf_op jit(solution)/shard_map/ppermute | solution.py:15
  21.3 1.3 %collective-permute-done.refs_6_.refs_3_ = bf16[288,384]{1,0:T(8,128)(2,1)S(1)} collective-permute-done((bf16[288,384]{1,0:T(8,128)(2,1)S(1)}, bf16[288,384]{1,0:T(8,128)(2,1)S(1)}, u32[]{:S(2)}, u32[]{:S(2)}) %collective-permute-start) | collective-permute-done | bytes 221216 | tf_op jit(solution)/shard_map/ppermute | solution.py:15
  22.6 6.3 %collective-permute-done.8.refs_5_ = bf16[48,2304]{1,0:T(8,128)(2,1)S(1)} collective-permute-done((bf16[48,2304]{1,0:T(8,128)(2,1)S(1)}, bf16[48,2304]{1,0:T(8,128)(2,1)S(1)}, u32[]{:S(2)}, u32[]{:S(2)}) %collective-permute-start.8) | collective-permute-done | bytes 221216 | tf_op jit(solution)/shard_map/ppermute | solution.py:15
  29.8 1.4 %collective-permute-start.10 = (bf16[48,2304]{1,0:T(8,128)(2,1)S(1)}, bf16[48,2304]{1,0:T(8,128)(2,1)}, u32[]{:S(2)}, u32[]{:S(2)}) collective-permute-start(bf16[48,2304]{1,0:T(8,128)(2,1)S(1)} %collective-permute-done.8.refs_5_), channel_id=1, source_target_pairs={{0,8},{4,12},{8,0},{12,4},{16,24},{20,28},{24,16},{28,20},{1,9},{5... | collective-permute-start | bytes 663560 | tf_op jit(solution)/shard_map/ppermute | solution.py:15
  32.6 1.8 %shard_map.101 = (f32[384,1152]{1,0:T(8,128)S(1)}, f32[384,1152]{1,0:T(8,128)S(1)}, bf16[768,1152]{1,0:T(8,128)(2,1)S(1)}, f32[2,384,128]{2,1,0:T(8,128)S(1)}) custom-call(bf16[768,640]{1,0:T(8,128)(2,1)S(1)} %shard_map.100.refs_0_, bf16[768,640]{1,0:T(8,128)(2,1)S(1)} %collective-permute-done.9.refs_1_), custom_call_target="tpu_custom_call" | custom-call | tf_op jit(solution)/shard_map/pallas_call | solution.py:213
  34.4 2.9 %collective-permute-done.10.refs_6_ = bf16[48,2304]{1,0:T(8,128)(2,1)} collective-permute-done((bf16[48,2304]{1,0:T(8,128)(2,1)S(1)}, bf16[48,2304]{1,0:T(8,128)(2,1)}, u32[]{:S(2)}, u32[]{:S(2)}) %collective-permute-start.10) | collective-permute-done | bytes 221216 | tf_op jit(solution)/shard_map/ppermute | solution.py:15
  37.3 2.5 %shard_map.102 = (bf16[384,1152]{1,0:T(8,128)(2,1)S(1)}, bf16[192,768]{1,0:T(8,128)(2,1)S(1)}, bf16[384,384]{1,0:T(8,128)(2,1)S(1)}) custom-call(s32[1]{0:T(128)} %bitcast.6.refs_0_, f32[2]{0:T(128)S(1)} %pad_maximum_fusion.refs_1_.refs_0_, bf16[768,1152]{1,0:T(8,128)(2,1)S(1)} %get-tuple-element.45.refs_2_.refs_1_, bf16[48,2304]{1,0:T(8,128)(2,1)S(1)} %shard_map.99.refs_3_, ...), custom_call_target="tpu_custom_call" | custom-call | tf_op jit(solution)/shard_map/pallas_call | solution.py:213
  39.9 3.3 %shard_map.103 = (f32[384,640]{1,0:T(8,128)S(1)}, f32[384,640]{1,0:T(8,128)}) custom-call(f32[2]{0:T(128)S(1)} %pad_maximum_fusion.refs_1_.refs_0_, f32[384,1152]{1,0:T(8,128)S(1)} %get-tuple-element.42.refs_1_, f32[384,1152]{1,0:T(8,128)S(1)} %get-tuple-element.43.refs_2_, f32[2,384,128]{2,1,0:T(8,128)S(1)} %get-tuple-element.44.refs_3_, ...), custom_call_target="tpu_custom_call" | custom-call | tf_op jit(solution)/shard_map/pallas_call | solution.py:213
  43.1 2.9 %shard_map.104 = (f32[48,1152]{1,0:T(8,128)S(1)}, f32[48,1152]{1,0:T(8,128)S(1)}, bf16[96,1152]{1,0:T(8,128)(2,1)}) custom-call(f32[2]{0:T(128)S(1)} %pad_maximum_fusion.refs_1_.refs_0_, bf16[768,1152]{1,0:T(8,128)(2,1)S(1)} %get-tuple-element.45.refs_2_.refs_1_, bf16[192,768]{1,0:T(8,128)(2,1)S(1)} %get-tuple-element.50.refs_2_, ...), custom_call_target="tpu_custom_call" | custom-call | tf_op jit(solution)/shard_map/pallas_call | solution.py:213
  47.4 1.4 %collective-permute-start.19 = (bf16[96,1152]{1,0:T(8,128)(2,1)}, bf16[96,1152]{1,0:T(8,128)(2,1)}, u32[]{:S(2)}, u32[]{:S(2)}) collective-permute-start(bf16[96,1152]{1,0:T(8,128)(2,1)} %get-tuple-element.61), channel_id=1, source_target_pairs={{0,8},{4,12},{8,0},{12,4},{16,24},{20,28},{24,16},{28,20},{1,9},{5... | collective-permute-start | bytes 663560 | tf_op jit(solution)/shard_map/ppermute | solution.py:15
  50.0 1.6 %collective-permute-start.12 = (bf16[336,256]{1,0:T(8,128)(2,1)S(1)}, bf16[336,256]{1,0:T(8,128)(2,1)S(1)}, u32[]{:S(2)}, u32[]{:S(2)}) collective-permute-start(bf16[336,256]{1,0:T(8,128)(2,1)S(1)} %get-tuple-element.53), channel_id=1, source_target_pairs={{0,2},{1,3},{2,0},{3,1},{4,6},{5,7},{6,4},{7,5},{8,10},{9,11},{10,... | collective-permute-start | bytes 516104 | tf_op jit(solution)/shard_map/ppermute | solution.py:15
  51.5 1.4 %collective-permute-start.13 = (bf16[224,256]{1,0:T(8,128)(2,1)S(1)}, bf16[224,256]{1,0:T(8,128)(2,1)S(1)}, u32[]{:S(2)}, u32[]{:S(2)}) collective-permute-start(bf16[224,256]{1,0:T(8,128)(2,1)S(1)} %get-tuple-element.54), channel_id=1, source_target_pairs={{0,4},{4,0},{8,12},{12,8},{16,20},{20,16},{24,28},{28,24},{1,5},{5... | collective-permute-start | bytes 344072 | tf_op jit(solution)/shard_map/ppermute | solution.py:15
  53.5 2.0 %collective-permute-done.19.refs_2_ = bf16[96,1152]{1,0:T(8,128)(2,1)} collective-permute-done((bf16[96,1152]{1,0:T(8,128)(2,1)}, bf16[96,1152]{1,0:T(8,128)(2,1)}, u32[]{:S(2)}, u32[]{:S(2)}) %collective-permute-start.19) | collective-permute-done | bytes 221216 | tf_op jit(solution)/shard_map/ppermute | solution.py:15
  56.5 2.1 %collective-permute-start.20 = (bf16[48,1152]{1,0:T(8,128)(2,1)S(1)}, bf16[48,1152]{1,0:T(8,128)(2,1)S(1)}, u32[]{:S(2)}, u32[]{:S(2)}) collective-permute-start(bf16[48,1152]{1,0:T(8,128)(2,1)S(1)} %get-tuple-element.63), channel_id=1, source_target_pairs={{0,16},{4,20},{8,24},{12,28},{16,0},{20,4},{24,8},{28,12},{1,17},{... | collective-permute-start | bytes 331784 | tf_op jit(solution)/shard_map/ppermute | solution.py:15
  58.6 1.2 %collective-permute-done.14.refs_4_ = bf16[224,256]{1,0:T(8,128)(2,1)S(1)} collective-permute-done((bf16[224,256]{1,0:T(8,128)(2,1)S(1)}, bf16[224,256]{1,0:T(8,128)(2,1)S(1)}, u32[]{:S(2)}, u32[]{:S(2)}) %collective-permute-start.14) | collective-permute-done | bytes 114720 | tf_op jit(solution)/shard_map/ppermute | solution.py:699
  60.7 3.8 %collective-permute-done.20.refs_1_ = bf16[48,1152]{1,0:T(8,128)(2,1)S(1)} collective-permute-done((bf16[48,1152]{1,0:T(8,128)(2,1)S(1)}, bf16[48,1152]{1,0:T(8,128)(2,1)S(1)}, u32[]{:S(2)}, u32[]{:S(2)}) %collective-permute-start.20) | collective-permute-done | bytes 110624 | tf_op jit(solution)/shard_map/ppermute | solution.py:15
  64.7 1.6 %collective-permute-start.22 = (bf16[48,288]{1,0:T(8,128)(2,1)S(1)}, bf16[48,288]{1,0:T(8,128)(2,1)S(1)}, u32[]{:S(2)}, u32[]{:S(2)}) collective-permute-start(bf16[48,288]{1,0:T(8,128)(2,1)S(1)} %get-tuple-element.66), channel_id=1, source_target_pairs={{0,2},{1,3},{2,0},{3,1},{4,6},{5,7},{6,4},{7,5},{8,10},{9,11},{10,... | collective-permute-start | bytes 82952 | tf_op jit(solution)/shard_map/ppermute | solution.py:15
  66.6 1.2 %shard_map.107 = (f32[144,288]{1,0:T(8,128)S(1)}, bf16[176,256]{1,0:T(8,128)(2,1)S(1)}, bf16[176,256]{1,0:T(8,128)(2,1)S(1)}, bf16[176,256]{1,0:T(8,128)(2,1)S(1)}) custom-call(s32[1]{0:T(128)} %bitcast.refs_1_.refs_0_, s32[4]{0:T(128)S(1)} %iota_multiply_fusion.refs_0_.refs_1_, bf16[576,384]{1,0:T(8,128)(2,1)S(1)} %get-tuple-element.38.refs_2_, ...), custom_call_target="tpu_custom_call" | custom-call | tf_op jit(solution)/shard_map/pallas_call | solution.py:213
  69.8 1.4 %collective-permute-start.24 = (bf16[224,256]{1,0:T(8,128)(2,1)S(1)}, bf16[224,256]{1,0:T(8,128)(2,1)S(1)}, u32[]{:S(2)}, u32[]{:S(2)}) collective-permute-start(bf16[224,256]{1,0:T(8,128)(2,1)S(1)} %shard_map.111.refs_5_), channel_id=1, source_target_pairs={{0,4},{4,0},{8,12},{12,8},{16,20},{20,16},{24,28},{28,24},{1,5},{5... | collective-permute-start | bytes 344072 | tf_op jit(solution)/shard_map/ppermute | solution.py:15
  71.4 3.4 %collective-permute-start.17 = (bf16[176,256]{1,0:T(8,128)(2,1)S(1)}, bf16[176,256]{1,0:T(8,128)(2,1)S(1)}, u32[]{:S(2)}, u32[]{:S(2)}) collective-permute-start(bf16[176,256]{1,0:T(8,128)(2,1)S(1)} %get-tuple-element.58), channel_id=1, source_target_pairs={{0,16},{4,20},{8,24},{12,28},{16,0},{20,4},{24,8},{28,12},{1,17},{... | collective-permute-start | bytes 270344 | tf_op jit(solution)/shard_map/ppermute | solution.py:15
  75.6 1.2 %shard_map.112 = (f32[144,288]{1,0:T(8,128)S(1)}, bf16[176,256]{1,0:T(8,128)(2,1)S(1)}, bf16[176,256]{1,0:T(8,128)(2,1)S(1)}, bf16[176,256]{1,0:T(8,128)(2,1)S(1)}) custom-call(s32[1]{0:T(128)} %bitcast.refs_1_.refs_0_, s32[4]{0:T(128)S(1)} %xor_multiply_fusion.refs_0_.refs_1_, bf16[576,384]{1,0:T(8,128)(2,1)S(1)} %get-tuple-element.38.refs_2_, ...), custom_call_target="tpu_custom_call" | custom-call | tf_op jit(solution)/shard_map/pallas_call | solution.py:213
  76.9 3.5 %collective-permute-start.26 = (bf16[176,256]{1,0:T(8,128)(2,1)S(1)}, bf16[176,256]{1,0:T(8,128)(2,1)S(1)}, u32[]{:S(2)}, u32[]{:S(2)}) collective-permute-start(bf16[176,256]{1,0:T(8,128)(2,1)S(1)} %get-tuple-element.70), channel_id=1, source_target_pairs={{0,16},{4,20},{8,24},{12,28},{16,0},{20,4},{24,8},{28,12},{1,17},{... | collective-permute-start | bytes 270344 | tf_op jit(solution)/shard_map/ppermute | solution.py:15
  81.2 1.3 %collective-permute-done.17.refs_2_ = bf16[176,256]{1,0:T(8,128)(2,1)S(1)} collective-permute-done((bf16[176,256]{1,0:T(8,128)(2,1)S(1)}, bf16[176,256]{1,0:T(8,128)(2,1)S(1)}, u32[]{:S(2)}, u32[]{:S(2)}) %collective-permute-start.17) | collective-permute-done | bytes 90144 | tf_op jit(solution)/shard_map/ppermute | solution.py:15
  83.3 6.4 %collective-permute-done.26.refs_2_ = bf16[176,256]{1,0:T(8,128)(2,1)S(1)} collective-permute-done((bf16[176,256]{1,0:T(8,128)(2,1)S(1)}, bf16[176,256]{1,0:T(8,128)(2,1)S(1)}, u32[]{:S(2)}, u32[]{:S(2)}) %collective-permute-start.26) | collective-permute-done | bytes 90144 | tf_op jit(solution)/shard_map/ppermute | solution.py:15
  (69 shorter events, 16.7 us)
Async XLA Ops:
  0.6 7.5 %copy-start = (bf16[192,1152]{1,0:T(8,128)(2,1)S(1)}, bf16[192,1152]{1,0:T(8,128)(2,1)}, u32[]{:S(2)}) copy-start(bf16[192,1152]{1,0:T(8,128)(2,1)} %refs_2_.1) | copy-start | bytes 1327108
  3.9 4.2 %copy-start.7 = (bf16[1152,288]{0,1:T(8,128)(2,1)S(1)}, bf16[1152,288]{0,1:T(8,128)(2,1)}, u32[]{:S(2)}) copy-start(bf16[1152,288]{0,1:T(8,128)(2,1)} %param.10) | copy-start | bytes 1990660
  3.9 8.7 %copy-start.2 = (bf16[192,1152]{1,0:T(8,128)(2,1)S(1)}, bf16[192,1152]{1,0:T(8,128)(2,1)}, u32[]{:S(2)}) copy-start(bf16[192,1152]{1,0:T(8,128)(2,1)} %refs_3_.1) | copy-start | bytes 1327108
  5.1 7.4 %collective-permute-start.5 = (bf16[96,576]{1,0:T(8,128)(2,1)S(1)}, bf16[96,576]{1,0:T(8,128)(2,1)S(1)}, u32[]{:S(2)}, u32[]{:S(2)}) collective-permute-start(bf16[96,576]{1,0:T(8,128)(2,1)S(1)} %get-tuple-element.40), channel_id=1, source_target_pairs={{0,2},{1,3},{2,0},{3,1},{4,6},{5,7},{6,4},{7,5},{8,10},{9,11},{10,... | collective-permute-start | bytes 331784 | tf_op jit(solution)/shard_map/ppermute | solution.py:15
  10.4 9.4 %collective-permute-start.2 = (bf16[192,576]{1,0:T(8,128)(2,1)S(1)}, bf16[192,576]{1,0:T(8,128)(2,1)S(1)}, u32[]{:S(2)}, u32[]{:S(2)}) collective-permute-start(bf16[192,576]{1,0:T(8,128)(2,1)S(1)} %shard_map.96.refs_4_.refs_0_), channel_id=1, source_target_pairs={{0,4},{4,0},{8,12},{12,8},{16,20},{20,16},{24,28},{28,24},{1,5},{5... | collective-permute-start | bytes 663560 | tf_op jit(solution)/shard_map/ppermute | solution.py:15
  12.0 9.3 %collective-permute-start.3 = (bf16[192,576]{1,0:T(8,128)(2,1)S(1)}, bf16[192,576]{1,0:T(8,128)(2,1)S(1)}, u32[]{:S(2)}, u32[]{:S(2)}) collective-permute-start(bf16[192,576]{1,0:T(8,128)(2,1)S(1)} %shard_map.96.refs_4_.refs_0_), channel_id=1, source_target_pairs={{0,2},{1,3},{2,0},{3,1},{4,6},{5,7},{6,4},{7,5},{8,10},{9,11},{10,... | collective-permute-start | bytes 663560 | tf_op jit(solution)/shard_map/ppermute | solution.py:15
  12.6 2.9 %collective-permute-start.6 = (bf16[96,576]{1,0:T(8,128)(2,1)S(1)}, bf16[96,576]{1,0:T(8,128)(2,1)S(1)}, u32[]{:S(2)}, u32[]{:S(2)}) collective-permute-start(bf16[96,576]{1,0:T(8,128)(2,1)S(1)} %shard_map.98), channel_id=1, source_target_pairs={{0,1},{1,0},{2,3},{3,2},{4,5},{5,4},{6,7},{7,6},{8,9},{9,8},{10,11... | collective-permute-start | bytes 331784 | tf_op jit(solution)/shard_map/ppermute | solution.py:15
  14.8 7.9 %collective-permute-start = (bf16[288,384]{1,0:T(8,128)(2,1)S(1)}, bf16[288,384]{1,0:T(8,128)(2,1)S(1)}, u32[]{:S(2)}, u32[]{:S(2)}) collective-permute-start(bf16[288,384]{1,0:T(8,128)(2,1)S(1)} %get-tuple-element.39), channel_id=1, source_target_pairs={{0,4},{4,0},{8,12},{12,8},{16,20},{20,16},{24,28},{28,24},{1,5},{5... | collective-permute-start | bytes 663560 | tf_op jit(solution)/shard_map/ppermute | solution.py:15
  15.6 13.3 %collective-permute-start.8 = (bf16[48,2304]{1,0:T(8,128)(2,1)S(1)}, bf16[48,2304]{1,0:T(8,128)(2,1)S(1)}, u32[]{:S(2)}, u32[]{:S(2)}) collective-permute-start(bf16[48,2304]{1,0:T(8,128)(2,1)S(1)} %shard_map.99.refs_3_), channel_id=1, source_target_pairs={{0,16},{4,20},{8,24},{12,28},{16,0},{20,4},{24,8},{28,12},{1,17},{... | collective-permute-start | bytes 663560 | tf_op jit(solution)/shard_map/ppermute | solution.py:15
  18.3 10.9 %collective-permute-start.7 = (bf16[48,2304]{1,0:T(8,128)(2,1)S(1)}, bf16[48,2304]{1,0:T(8,128)(2,1)S(1)}, u32[]{:S(2)}, u32[]{:S(2)}) collective-permute-start(bf16[48,2304]{1,0:T(8,128)(2,1)S(1)} %shard_map.99.refs_3_), channel_id=1, source_target_pairs={{0,8},{4,12},{8,0},{12,4},{16,24},{20,28},{24,16},{28,20},{1,9},{5... | collective-permute-start | bytes 663560 | tf_op jit(solution)/shard_map/ppermute | solution.py:15
  19.8 9.3 %collective-permute-start.4 = (bf16[192,576]{1,0:T(8,128)(2,1)S(1)}, bf16[192,576]{1,0:T(8,128)(2,1)S(1)}, u32[]{:S(2)}, u32[]{:S(2)}) collective-permute-start(bf16[192,576]{1,0:T(8,128)(2,1)S(1)} %collective-permute-done.2.refs_1_), channel_id=1, source_target_pairs={{0,2},{1,3},{2,0},{3,1},{4,6},{5,7},{6,4},{7,5},{8,10},{9,11},{10,... | collective-permute-start | bytes 663560 | tf_op jit(solution)/shard_map/ppermute | solution.py:15
  29.2 3.4 %collective-permute-start.9 = (bf16[768,640]{1,0:T(8,128)(2,1)S(1)}, bf16[768,640]{1,0:T(8,128)(2,1)S(1)}, u32[]{:S(2)}, u32[]{:S(2)}) collective-permute-start(bf16[768,640]{1,0:T(8,128)(2,1)S(1)} %shard_map.100.refs_0_), channel_id=1, source_target_pairs={{0,1},{1,0},{2,3},{3,2},{4,5},{5,4},{6,7},{7,6},{8,9},{9,8},{10,11... | collective-permute-start | bytes 2949128 | tf_op jit(solution)/shard_map/ppermute | solution.py:15
  29.3 5.1 %collective-permute-start.1 = (bf16[288,384]{1,0:T(8,128)(2,1)S(1)}, bf16[288,384]{1,0:T(8,128)(2,1)S(1)}, u32[]{:S(2)}, u32[]{:S(2)}) collective-permute-start(bf16[288,384]{1,0:T(8,128)(2,1)S(1)} %collective-permute-done.refs_6_.refs_3_), channel_id=1, source_target_pairs={{0,1},{1,0},{2,3},{3,2},{4,5},{5,4},{6,7},{7,6},{8,9},{9,8},{10,11... | collective-permute-start | bytes 663560 | tf_op jit(solution)/shard_map/ppermute | solution.py:15
  29.8 7.5 %collective-permute-start.10 = (bf16[48,2304]{1,0:T(8,128)(2,1)S(1)}, bf16[48,2304]{1,0:T(8,128)(2,1)}, u32[]{:S(2)}, u32[]{:S(2)}) collective-permute-start(bf16[48,2304]{1,0:T(8,128)(2,1)S(1)} %collective-permute-done.8.refs_5_), channel_id=1, source_target_pairs={{0,8},{4,12},{8,0},{12,4},{16,24},{20,28},{24,16},{28,20},{1,9},{5... | collective-permute-start | bytes 663560 | tf_op jit(solution)/shard_map/ppermute | solution.py:15
  43.1 5.7 %collective-permute-start.11 = (f32[384,640]{1,0:T(8,128)}, f32[384,640]{1,0:T(8,128)S(1)}, u32[]{:S(2)}, u32[]{:S(2)}) collective-permute-start(f32[384,640]{1,0:T(8,128)} %get-tuple-element.49), channel_id=1, source_target_pairs={{0,1},{1,0},{2,3},{3,2},{4,5},{5,4},{6,7},{7,6},{8,9},{9,8},{10,11... | collective-permute-start | bytes 2949128 | tf_op jit(solution)/shard_map/ppermute | solution.py:15
  47.4 8.2 %collective-permute-start.19 = (bf16[96,1152]{1,0:T(8,128)(2,1)}, bf16[96,1152]{1,0:T(8,128)(2,1)}, u32[]{:S(2)}, u32[]{:S(2)}) collective-permute-start(bf16[96,1152]{1,0:T(8,128)(2,1)} %get-tuple-element.61), channel_id=1, source_target_pairs={{0,8},{4,12},{8,0},{12,4},{16,24},{20,28},{24,16},{28,20},{1,9},{5... | collective-permute-start | bytes 663560 | tf_op jit(solution)/shard_map/ppermute | solution.py:15
  49.8 5.8 %copy-start.10 = (f32[48,1152]{1,0:T(8,128)S(1)}, f32[48,1152]{1,0:T(8,128)}, u32[]{:S(2)}) copy-start(f32[48,1152]{1,0:T(8,128)} %copy-done.9) | copy-start | bytes 663556
  50.0 9.8 %collective-permute-start.12 = (bf16[336,256]{1,0:T(8,128)(2,1)S(1)}, bf16[336,256]{1,0:T(8,128)(2,1)S(1)}, u32[]{:S(2)}, u32[]{:S(2)}) collective-permute-start(bf16[336,256]{1,0:T(8,128)(2,1)S(1)} %get-tuple-element.53), channel_id=1, source_target_pairs={{0,2},{1,3},{2,0},{3,1},{4,6},{5,7},{6,4},{7,5},{8,10},{9,11},{10,... | collective-permute-start | bytes 516104 | tf_op jit(solution)/shard_map/ppermute | solution.py:15
  51.5 7.1 %collective-permute-start.13 = (bf16[224,256]{1,0:T(8,128)(2,1)S(1)}, bf16[224,256]{1,0:T(8,128)(2,1)S(1)}, u32[]{:S(2)}, u32[]{:S(2)}) collective-permute-start(bf16[224,256]{1,0:T(8,128)(2,1)S(1)} %get-tuple-element.54), channel_id=1, source_target_pairs={{0,4},{4,0},{8,12},{12,8},{16,20},{20,16},{24,28},{28,24},{1,5},{5... | collective-permute-start | bytes 344072 | tf_op jit(solution)/shard_map/ppermute | solution.py:15
  52.9 6.9 %collective-permute-start.14 = (bf16[224,256]{1,0:T(8,128)(2,1)S(1)}, bf16[224,256]{1,0:T(8,128)(2,1)S(1)}, u32[]{:S(2)}, u32[]{:S(2)}) collective-permute-start(bf16[224,256]{1,0:T(8,128)(2,1)S(1)} %get-tuple-element.55), channel_id=1, source_target_pairs={{0,6},{1,7},{2,4},{3,5},{4,2},{5,3},{6,0},{7,1},{8,14},{9,15},{10,... | collective-permute-start | bytes 344072 | tf_op jit(solution)/shard_map/ppermute | solution.py:699
  56.5 8.0 %collective-permute-start.20 = (bf16[48,1152]{1,0:T(8,128)(2,1)S(1)}, bf16[48,1152]{1,0:T(8,128)(2,1)S(1)}, u32[]{:S(2)}, u32[]{:S(2)}) collective-permute-start(bf16[48,1152]{1,0:T(8,128)(2,1)S(1)} %get-tuple-element.63), channel_id=1, source_target_pairs={{0,16},{4,20},{8,24},{12,28},{16,0},{20,4},{24,8},{28,12},{1,17},{... | collective-permute-start | bytes 331784 | tf_op jit(solution)/shard_map/ppermute | solution.py:15
  60.0 6.6 %collective-permute-start.15 = (bf16[224,256]{1,0:T(8,128)(2,1)S(1)}, bf16[224,256]{1,0:T(8,128)(2,1)S(1)}, u32[]{:S(2)}, u32[]{:S(2)}) collective-permute-start(bf16[224,256]{1,0:T(8,128)(2,1)S(1)} %shard_map.106.refs_5_.refs_2_), channel_id=1, source_target_pairs={{0,4},{4,0},{8,12},{12,8},{16,20},{20,16},{24,28},{28,24},{1,5},{5... | collective-permute-start | bytes 344072 | tf_op jit(solution)/shard_map/ppermute | solution.py:15
  64.6 3.1 %collective-permute-start.21 = (bf16[48,288]{1,0:T(8,128)(2,1)S(1)}, bf16[48,288]{1,0:T(8,128)(2,1)S(1)}, u32[]{:S(2)}, u32[]{:S(2)}) collective-permute-start(bf16[48,288]{1,0:T(8,128)(2,1)S(1)} %get-tuple-element.65), channel_id=1, source_target_pairs={{0,1},{1,0},{2,3},{3,2},{4,5},{5,4},{6,7},{7,6},{8,9},{9,8},{10,11... | collective-permute-start | bytes 82952 | tf_op jit(solution)/shard_map/ppermute | solution.py:15
  64.7 4.0 %collective-permute-start.22 = (bf16[48,288]{1,0:T(8,128)(2,1)S(1)}, bf16[48,288]{1,0:T(8,128)(2,1)S(1)}, u32[]{:S(2)}, u32[]{:S(2)}) collective-permute-start(bf16[48,288]{1,0:T(8,128)(2,1)S(1)} %get-tuple-element.66), channel_id=1, source_target_pairs={{0,2},{1,3},{2,0},{3,1},{4,6},{5,7},{6,4},{7,5},{8,10},{9,11},{10,... | collective-permute-start | bytes 82952 | tf_op jit(solution)/shard_map/ppermute | solution.py:15
  66.3 3.4 %collective-permute-start.23 = (bf16[48,288]{1,0:T(8,128)(2,1)S(1)}, bf16[48,288]{1,0:T(8,128)(2,1)S(1)}, u32[]{:S(2)}, u32[]{:S(2)}) collective-permute-start(bf16[48,288]{1,0:T(8,128)(2,1)S(1)} %get-tuple-element.67), channel_id=1, source_target_pairs={{0,3},{1,2},{2,1},{3,0},{4,7},{5,6},{6,5},{7,4},{8,11},{9,10},{10,... | collective-permute-start | bytes 82952 | tf_op jit(solution)/shard_map/ppermute | solution.py:15
  69.8 5.8 %collective-permute-start.24 = (bf16[224,256]{1,0:T(8,128)(2,1)S(1)}, bf16[224,256]{1,0:T(8,128)(2,1)S(1)}, u32[]{:S(2)}, u32[]{:S(2)}) collective-permute-start(bf16[224,256]{1,0:T(8,128)(2,1)S(1)} %shard_map.111.refs_5_), channel_id=1, source_target_pairs={{0,4},{4,0},{8,12},{12,8},{16,20},{20,16},{24,28},{28,24},{1,5},{5... | collective-permute-start | bytes 344072 | tf_op jit(solution)/shard_map/ppermute | solution.py:15
  71.2 9.1 %collective-permute-start.16 = (bf16[176,256]{1,0:T(8,128)(2,1)S(1)}, bf16[176,256]{1,0:T(8,128)(2,1)S(1)}, u32[]{:S(2)}, u32[]{:S(2)}) collective-permute-start(bf16[176,256]{1,0:T(8,128)(2,1)S(1)} %get-tuple-element.57), channel_id=1, source_target_pairs={{0,8},{4,12},{8,0},{12,4},{16,24},{20,28},{24,16},{28,20},{1,9},{5... | collective-permute-start | bytes 270344 | tf_op jit(solution)/shard_map/ppermute | solution.py:15
  71.4 11.1 %collective-permute-start.17 = (bf16[176,256]{1,0:T(8,128)(2,1)S(1)}, bf16[176,256]{1,0:T(8,128)(2,1)S(1)}, u32[]{:S(2)}, u32[]{:S(2)}) collective-permute-start(bf16[176,256]{1,0:T(8,128)(2,1)S(1)} %get-tuple-element.58), channel_id=1, source_target_pairs={{0,16},{4,20},{8,24},{12,28},{16,0},{20,4},{24,8},{28,12},{1,17},{... | collective-permute-start | bytes 270344 | tf_op jit(solution)/shard_map/ppermute | solution.py:15
  74.7 7.8 %collective-permute-start.18 = (bf16[176,256]{1,0:T(8,128)(2,1)S(1)}, bf16[176,256]{1,0:T(8,128)(2,1)S(1)}, u32[]{:S(2)}, u32[]{:S(2)}) collective-permute-start(bf16[176,256]{1,0:T(8,128)(2,1)S(1)} %get-tuple-element.59), channel_id=1, source_target_pairs={{0,24},{4,28},{8,16},{12,20},{16,8},{20,12},{24,0},{28,4},{1,25},{... | collective-permute-start | bytes 270344 | tf_op jit(solution)/shard_map/ppermute | solution.py:15
  76.8 6.5 %collective-permute-start.25 = (bf16[176,256]{1,0:T(8,128)(2,1)S(1)}, bf16[176,256]{1,0:T(8,128)(2,1)S(1)}, u32[]{:S(2)}, u32[]{:S(2)}) collective-permute-start(bf16[176,256]{1,0:T(8,128)(2,1)S(1)} %get-tuple-element.69), channel_id=1, source_target_pairs={{0,8},{4,12},{8,0},{12,4},{16,24},{20,28},{24,16},{28,20},{1,9},{5... | collective-permute-start | bytes 270344 | tf_op jit(solution)/shard_map/ppermute | solution.py:15
  76.9 12.8 %collective-permute-start.26 = (bf16[176,256]{1,0:T(8,128)(2,1)S(1)}, bf16[176,256]{1,0:T(8,128)(2,1)S(1)}, u32[]{:S(2)}, u32[]{:S(2)}) collective-permute-start(bf16[176,256]{1,0:T(8,128)(2,1)S(1)} %get-tuple-element.70), channel_id=1, source_target_pairs={{0,16},{4,20},{8,24},{12,28},{16,0},{20,4},{24,8},{28,12},{1,17},{... | collective-permute-start | bytes 270344 | tf_op jit(solution)/shard_map/ppermute | solution.py:15
  80.3 9.3 %collective-permute-start.27 = (bf16[176,256]{1,0:T(8,128)(2,1)S(1)}, bf16[176,256]{1,0:T(8,128)(2,1)S(1)}, u32[]{:S(2)}, u32[]{:S(2)}) collective-permute-start(bf16[176,256]{1,0:T(8,128)(2,1)S(1)} %get-tuple-element.71), channel_id=1, source_target_pairs={{0,24},{4,28},{8,16},{12,20},{16,8},{20,12},{24,0},{28,4},{1,25},{... | collective-permute-start | bytes 270344 | tf_op jit(solution)/shard_map/ppermute | solution.py:15
  (7 other events, 6.6 us)
